TPU v7x, 512 devices: a whole 4x4x16 slice. The times are simulated.
512 devices in a mesh: seq: 32 (over z_lo, y, core), chan: 4 (over z_hi), dp: 4 (over x).
Axes of the slice: x: 4, y: 4, z: 16 (z_hi: 4, z_lo: 4; z = z_hi * 4 + z_lo), core: 2. Of those that a mesh axis runs over, the one named last changes fastest.
Arguments:
- inputs: bfloat16 [4, 65536, 1024], P('dp', 'seq', 'chan'), may hold values from -6 to 6
- w_value: bfloat16 [4, 256, 256], P('chan'), may hold values from -0.375 to 0.375
- w_gate: bfloat16 [4, 256, 256], P('chan'), may hold values from -0.375 to 0.375
- w_out: bfloat16 [4, 256, 256], P('chan'), may hold values from -0.375 to 0.375
- mon_right: bfloat16 [256, 256], replicated, may hold values from -0.375 to 0.375
- mon_left: bfloat16 [256, 256], replicated, may hold values from -0.375 to 0.375
- twiddle: float32 [256, 256], P('seq'), may hold values from 0.4 to 1.6
- cotangent: bfloat16 [4, 65536, 1024], P('dp', 'seq', 'chan'), may hold values from -6 to 6
Outputs:
- grad_inputs: bfloat16 [4, 65536, 1024], P('dp', 'seq', 'chan')
- grad_value: float32 [4, 256, 256], P('chan')
- grad_gate: float32 [4, 256, 256], P('chan')
- grad_out: float32 [4, 256, 256], P('chan')
- grad_right: float32 [256, 256], replicated
- grad_left: float32 [256, 256], replicated
- grad_twiddle: float32 [256, 256], P('seq')
All inputs are finite; a program needn't handle non-finite values.
Results may differ from a plain program's by a relative error of at most 0.015.
Values may be sent and summed in bfloat16 or wider, within the bound.
No kernel may reach another device: no remote copies, remote signals or barrier semaphores. Data moves between devices by JAX's collectives and lax.ppermute only.
A program may use at most 64 MiB of HBM per device.

v0:
```python
import jax
import jax.numpy as jnp
from jax import lax
from jax.sharding import PartitionSpec as P


def channel_product(input_activations, weight_matrix):
    return jnp.einsum(
        "nfj,jr->nfr", input_activations, weight_matrix, preferred_element_type=jnp.float32
    )


def channel_back(input_activations, weight_matrix):
    return jnp.einsum(
        "bxj,rj->bxr", input_activations, weight_matrix, preferred_element_type=jnp.float32
    )


def across_blocks(left_factor, columns):
    return jnp.einsum(
        "ik,skjc->sijc", left_factor, columns, preferred_element_type=jnp.float32
    ).astype(jnp.bfloat16)


def across_back(left_factor, columns):
    return jnp.einsum(
        "ik,sijc->skjc", left_factor, columns, preferred_element_type=jnp.float32
    ).astype(jnp.bfloat16)


def on_device(inputs, w_value, w_gate, w_out, mon_right, mon_left, twiddle, cotangent):
    seq_count, local_len, width = inputs.shape
    block_size = mon_right.shape[0]
    local_blocks = local_len // block_size
    value_weight = w_value[0]
    gate_weight = w_gate[0]
    out_weight = w_out[0]
    values = channel_product(inputs, value_weight).astype(jnp.bfloat16)
    gates = channel_product(inputs, gate_weight).astype(jnp.bfloat16)
    cube = values.reshape(seq_count, local_blocks, block_size, width)
    rotated = jnp.einsum("jk,sikc->sijc", mon_right, cube, preferred_element_type=jnp.float32)
    twist_rows = twiddle[None, :, :, None]
    twisted = (rotated * twist_rows).astype(jnp.bfloat16)
    back_gated = channel_back(cotangent, out_weight).astype(jnp.bfloat16)
    back_mixed = (back_gated.astype(jnp.float32) * gates.astype(jnp.float32)).astype(jnp.bfloat16)
    back_cube = back_mixed.reshape(seq_count, local_blocks, block_size, width)
    twist_cols = lax.all_to_all(twisted, "seq", split_axis=2, concat_axis=1, tiled=True)
    mixed_cols = across_blocks(mon_left, twist_cols)
    mixed_cube = lax.all_to_all(mixed_cols, "seq", split_axis=1, concat_axis=2, tiled=True)
    back_cols = lax.all_to_all(back_cube, "seq", split_axis=2, concat_axis=1, tiled=True)
    back_twist_cols = across_back(mon_left, back_cols)
    back_twisted = lax.all_to_all(back_twist_cols, "seq", split_axis=1, concat_axis=2, tiled=True)
    left_part = jnp.einsum(
        "sijc,skjc->ik", back_cols, twist_cols, preferred_element_type=jnp.float32
    )
    mixed = mixed_cube.reshape(seq_count, local_len, width)
    gated_values = (gates.astype(jnp.float32) * mixed.astype(jnp.float32)).astype(jnp.bfloat16)
    output_block_weight = jnp.einsum(
        "yrz,yrj->zj", gated_values, cotangent, preferred_element_type=jnp.float32
    )
    gate_cotangents = (back_gated.astype(jnp.float32) * mixed.astype(jnp.float32)).astype(
        jnp.bfloat16
    )
    back_twist32 = back_twisted.astype(jnp.float32)
    twiddle_part = jnp.sum(back_twist32 * rotated, axis=(0, 3))
    back_rotated = (back_twist32 * twist_rows).astype(jnp.bfloat16)
    value_cotangents = jnp.einsum(
        "jk,sijc->sikc", mon_right, back_rotated, preferred_element_type=jnp.float32
    ).astype(jnp.bfloat16)
    right_part = jnp.einsum("sijc,sikc->jk", back_rotated, cube, preferred_element_type=jnp.float32)
    value_cotangents = value_cotangents.reshape(seq_count, local_len, width)
    grad_inputs = (
        channel_back(value_cotangents, value_weight) + channel_back(gate_cotangents, gate_weight)
    ).astype(jnp.bfloat16)
    value_block_weight = jnp.einsum(
        "yrz,yrj->zj", inputs, value_cotangents, preferred_element_type=jnp.float32
    )
    gate_block_weight = jnp.einsum(
        "yrz,yrj->zj", inputs, gate_cotangents, preferred_element_type=jnp.float32
    )
    value_sum, gate_sum, out_sum = lax.psum(
        (value_block_weight, gate_block_weight, output_block_weight), ("seq", "dp")
    )
    right_sum, left_sum = lax.psum((right_part, left_part), ("seq", "chan", "dp"))
    twiddle_sum = lax.psum(twiddle_part, ("chan", "dp"))
    return (
        grad_inputs,
        value_sum[None],
        gate_sum[None],
        out_sum[None],
        right_sum,
        left_sum,
        twiddle_sum,
    )


def solution(mesh):
    return jax.shard_map(
        on_device,
        mesh=mesh,
        in_specs=(
            P("dp", "seq", "chan"),
            P("chan", None, None),
            P("chan", None, None),
            P("chan", None, None),
            P(),
            P(),
            P("seq", None),
            P("dp", "seq", "chan"),
        ),
        out_specs=(
            P("dp", "seq", "chan"),
            P("chan", None, None),
            P("chan", None, None),
            P("chan", None, None),
            P(),
            P(),
            P("seq", None),
        ),
        check_vma=False,
    )
```

profile of v0, /device:TPU:1, one launch (start us, length us, event | category | flops | bytes accessed | tf_op | source)
XLA Modules:
  0.0 1913.4 jit_solution(14822535923958613904)
XLA Ops:
  7.2 1.8 convolution_convert_fusion.2
  9.0 1.4 fusion.3
  10.4 0.6 copy.58
  11.0 36.6 %all_to_all.48 = bf16[1,8,256,256]{3,1,0,2:T(8,128)(2,1)S(1)} all-to-all(bf16[1,8,256,256]{3,1,0,2:T(8,128)(2,1)S(1)} %copy.58), channel_id=1, replica_groups=mesh['seq'=32,'chan'=4,'dp'=4] {'seq'}, dimensions={2} | all-to-all | bytes 2097152 | tf_op jit(solution)/shard_map/all_to_all | solution.py:50
  47.6 0.2 copy.98
  47.8 0.1 copy.60
  47.9 1.0 copy-done.9
  48.9 0.5 fusion.8
  49.4 1.8 copy.62
  51.2 5.2 all-to-all-start.1
  56.5 1.4 convolution_convert_fusion
  57.9 25.2 %all-to-all-done.1 = bf16[1,256,8,256]{3,2,0,1:T(8,128)(2,1)S(1)} async-done(((bf16[1,256,8,256]{3,2,0,1:T(8,128)(2,1)}), bf16[1,256,8,256]{3,2,0,1:T(8,128)(2,1)S(1)}, u32[]{:S(2)}, u32[]{:S(2)}) %all-to-all-start.1) | async-done | bytes 1048608 | tf_op jit(solution)/shard_map/all_to_all | solution.py:52
  83.0 1.6 copy_bitcast_fusion
  84.7 2.9 copy.77
  87.6 3.5 fusion.6
  91.0 2.6 copy.67
  93.7 31.8 %all_to_all.49 = bf16[1,8,256,256]{3,1,0,2:T(8,128)(2,1)S(1)} all-to-all(bf16[1,8,256,256]{3,1,0,2:T(8,128)(2,1)} %copy.67), channel_id=1, replica_groups=mesh['seq'=32,'chan'=4,'dp'=4] {'seq'}, dimensions={2} | all-to-all | bytes 2097152 | tf_op jit(solution)/shard_map/all_to_all | solution.py:47
  125.5 0.2 copy.97
  125.7 0.1 copy.69
  125.8 1.0 copy-done.6
  126.8 1.5 fusion.9
  128.3 2.7 copy.71
  131.0 5.3 all-to-all-start.3
  136.3 0.0 all-reduce.7.cloned.1.call-start
  136.3 0.8 convolution_convert_fusion.4
  137.1 1.0 copy-done.3
  138.1 1.2 convolution_bitcast_fusion.4
  139.3 23.6 %all-to-all-done.3 = bf16[1,256,8,256]{3,2,0,1:T(8,128)(2,1)} async-done(((bf16[1,256,8,256]{3,2,0,1:T(8,128)(2,1)}), bf16[1,256,8,256]{3,2,0,1:T(8,128)(2,1)}, u32[]{:S(2)}, u32[]{:S(2)}) %all-to-all-start.3) | async-done | bytes 1048608 | tf_op jit(solution)/shard_map/all_to_all | solution.py:49
  162.9 1.5 convert_bitcast_fusion
  164.4 0.2 copy.73
  164.6 1.0 copy-done.8
  165.6 0.5 fusion.4
  166.1 1.2 convolution_bitcast_fusion.3
  167.3 0.0 copy-done.5
  167.3 1.2 convolution_bitcast_fusion.2
  168.6 0.0 all-reduce.5.cloned.1.call-start
  168.6 2.6 convolution_bitcast_fusion.1
  171.2 1.4 convolution_bitcast_fusion
  172.6 1.8 fusion.23
  174.4 50.5 %psum.47 = f32[8,256]{1,0:T(8,128)} all-reduce(f32[8,256]{1,0:T(8,128)S(1)} %get-tuple-element.40), channel_id=1, replica_groups=mesh['seq'=32,'chan'=4,'dp'=4] {'chan','dp'}, use_global_device_ids=true, to_apply=%region_6.0 | all-reduce | flops 2048 | bytes 16384 | tf_op jit(solution)/shard_map/psum | solution.py:85
  224.9 3.0 fusion.1
  228.0 1209.2 %all-reduce.7.cloned.1.call-done = (f32[1,256,256]{1,2,0:T(8,128)}, f32[1,256,256]{1,2,0:T(8,128)}, f32[1,256,256]{2,1,0:T(8,128)}) async-done(((f32[1,256,256]{1,2,0:T(8,128)}, f32[1,256,256]{1,2,0:T(8,128)}, f32[1,256,256]{2,1,0:T(8,128)}), (f32[1,256,256]{1,2,0:T(8,128)}, f32[1,256,256]{1,2,0:T(8,128)}, f32[1,256,256]{2,1,0:T(8,128)})) %all-reduce.7.cloned.1.call-update) | async-done | bytes 786448 | tf_op jit(solution)/shard_map/psum | solution.py:81
  1437.2 1.8 copy.78
  1439.0 1.8 copy.79
  1440.8 460.8 %all-reduce.5.cloned.1.call-done = (f32[256,256]{1,0:T(8,128)}, f32[256,256]{1,0:T(8,128)}) async-done(((f32[256,256]{1,0:T(8,128)}, f32[256,256]{1,0:T(8,128)}), (f32[256,256]{1,0:T(8,128)}, f32[256,256]{1,0:T(8,128)})) %all-reduce.5.cloned.1.call-update) | async-done | bytes 524304 | tf_op jit(solution)/shard_map/psum | solution.py:84
  1901.5 1.7 copy.104
  1903.2 1.7 copy.105
  1904.9 1.7 copy.106
  (29 shorter events, 0.1 us)
Async XLA Ops:
  7.2 1.8 copy-start
  7.2 1.8 copy-start.12
  47.6 1.3 copy-start.13
  47.9 1.0 copy-start.9
  49.4 7.0 copy-start.11
  51.2 31.8 %all-to-all-start.1 = ((bf16[1,256,8,256]{3,2,0,1:T(8,128)(2,1)}), bf16[1,256,8,256]{3,2,0,1:T(8,128)(2,1)S(1)}, u32[]{:S(2)}, u32[]{:S(2)}) async-start(bf16[1,256,8,256]{3,2,0,1:T(8,128)(2,1)} %copy.62), calls=%async_computation.1 | async-start | bytes 2097152 | tf_op jit(solution)/shard_map/all_to_all | solution.py:52
  83.0 53.3 %copy-start.1 = (bf16[1,256,8,256]{3,2,0,1:T(8,128)(2,1)}, bf16[1,256,8,256]{3,2,0,1:T(8,128)(2,1)S(1)}, u32[]{:S(2)}) copy-start(bf16[1,256,8,256]{3,2,0,1:T(8,128)(2,1)S(1)} %all-to-all-done.1) | copy-start | bytes 3145732
  84.7 2.9 copy-start.15
  125.8 1.0 copy-start.6
  128.3 8.0 copy-start.14
  131.0 31.9 %all-to-all-start.3 = ((bf16[1,256,8,256]{3,2,0,1:T(8,128)(2,1)}), bf16[1,256,8,256]{3,2,0,1:T(8,128)(2,1)}, u32[]{:S(2)}, u32[]{:S(2)}) async-start(bf16[1,256,8,256]{3,2,0,1:T(8,128)(2,1)} %copy.71), calls=%async_computation.3 | async-start | bytes 2097152 | tf_op jit(solution)/shard_map/all_to_all | solution.py:49
  136.3 1300.9 %all-reduce.7.cloned.1.call-start = ((), (), s32[]{:S(2)}) async-start(), calls=%async_computation.5 | async-start | bytes 1572864 | tf_op jit(solution)/shard_map/psum | solution.py:81
  137.1 1.0 copy-start.3
  164.4 1.2 copy-start.8
  166.1 1.2 copy-start.5
  167.3 1.3 copy-start.2
  168.6 1733.0 %all-reduce.5.cloned.1.call-start = ((), (), s32[]{:S(2)}) async-start(), calls=%async_computation.4 | async-start | bytes 1048576 | tf_op jit(solution)/shard_map/psum | solution.py:84
  168.6 2.6 copy-start.7
  168.6 2.6 copy-start.10
  171.2 1.4 copy-start.4
Sparse Core Ops, SparseCore 0:
  168.7 1268.4 all-reduce.6
  1443.6 457.9 all-reduce.4
where the time goes:
time: 1910 us
  waiting for transfers between devices  1720 us (90%)
  blocking collectives  119 us (6%)
  local copies, waits for them, and re-layouts  24 us (1%)
  matrix products  23.2 us (1%)
    psum x1, waiting for transfers between devices, on_device(): lax.psum((value_block_weight, gate_block_weight, output_block_weight), ('...  1210 us
    psum x1, waiting for transfers between devices, on_device(): lax.psum((right_part, left_part), ('seq', 'chan', 'dp'))  461 us
    psum x1, blocking collectives, on_device(): twiddle_sum = lax.psum(twiddle_part, ('chan', 'dp'))  50.5 us
  transfers between devices with their start and end apart: 4, of which 4 were waited for; matrix products, arithmetic and copies ran while one was open for 1% of the time, Pallas kernels for 0%

commit v1 on v0

v1 whole, which is shorter than its diff:
```python
import jax
import jax.numpy as jnp
from jax import lax
from jax.sharding import PartitionSpec as P

F32 = jnp.float32
BF16 = jnp.bfloat16


def channel_product(rows, weight):
    return jnp.einsum("nfj,jr->nfr", rows, weight, preferred_element_type=F32)


def channel_back(rows, weight):
    return jnp.einsum("bxj,rj->bxr", rows, weight, preferred_element_type=F32)


def across_blocks(left_factor, columns):
    return jnp.einsum(
        "ik,skjc->sijc", left_factor, columns, preferred_element_type=F32
    ).astype(BF16)


def across_back(left_factor, columns):
    return jnp.einsum(
        "ik,sijc->skjc", left_factor, columns, preferred_element_type=F32
    ).astype(BF16)


def swap(array, axis, size, step):
    return lax.ppermute(array, axis, [(i, i ^ step) for i in range(size)])


def scatter_sum(parts, axis):
    size = parts.shape[0]
    me = lax.axis_index(axis)
    total = lax.dynamic_index_in_dim(parts, me, 0, keepdims=False).astype(F32)
    for step in range(1, size):
        out = lax.dynamic_index_in_dim(parts, me ^ step, 0, keepdims=False)
        total = total + swap(out, axis, size, step).astype(F32)
    return total


def exchange_sum(array, axis, size):
    one, two, three = (swap(array, axis, size, step) for step in (1, 2, 3))
    return (array + one) + (two + three)


def gather(array, axis, size):
    me = lax.axis_index(axis)
    out = jnp.zeros((size,) + array.shape, array.dtype)
    for step in range(size):
        part = array if step == 0 else swap(array, axis, size, step)
        out = lax.dynamic_update_index_in_dim(out, part, me ^ step, 0)
    return out


def on_device(sizes, inputs, w_value, w_gate, w_out, mon_right, mon_left, twiddle, cotangent):
    seq_size, chan_size, dp_size = sizes
    seq_count, local_len, width = inputs.shape
    block_size = mon_right.shape[0]
    local_blocks = local_len // block_size
    value_weight = w_value[0]
    gate_weight = w_gate[0]
    out_weight = w_out[0]
    gates = channel_product(inputs, gate_weight).astype(BF16)
    back_gated = channel_back(cotangent, out_weight).astype(BF16)
    back_mixed = (back_gated.astype(F32) * gates.astype(F32)).astype(BF16)
    back_cube = back_mixed.reshape(seq_count, local_blocks, block_size, width)
    back_cols = lax.all_to_all(back_cube, "seq", split_axis=2, concat_axis=1, tiled=True)
    values = channel_product(inputs, value_weight).astype(BF16)
    cube = values.reshape(seq_count, local_blocks, block_size, width)
    rotated = jnp.einsum("jk,sikc->sijc", mon_right, cube, preferred_element_type=F32)
    twist_rows = twiddle[None, :, :, None]
    twisted = (rotated * twist_rows).astype(BF16)
    twist_cols = lax.all_to_all(twisted, "seq", split_axis=2, concat_axis=1, tiled=True)
    back_twist_cols = across_back(mon_left, back_cols)
    back_twisted = lax.all_to_all(back_twist_cols, "seq", split_axis=1, concat_axis=2, tiled=True)
    mixed_cols = across_blocks(mon_left, twist_cols)
    mixed_cube = lax.all_to_all(mixed_cols, "seq", split_axis=1, concat_axis=2, tiled=True)
    left_part = jnp.einsum("sijc,skjc->ik", back_cols, twist_cols, preferred_element_type=F32)
    back_twist32 = back_twisted.astype(F32)
    twiddle_part = jnp.sum(back_twist32 * rotated, axis=(0, 3))
    back_rotated = (back_twist32 * twist_rows).astype(BF16)
    value_cotangents = jnp.einsum(
        "jk,sijc->sikc", mon_right, back_rotated, preferred_element_type=F32
    ).astype(BF16)
    right_part = jnp.einsum("sijc,sikc->jk", back_rotated, cube, preferred_element_type=F32)
    value_cotangents = value_cotangents.reshape(seq_count, local_len, width)
    value_part = jnp.einsum("yrz,yrj->zj", inputs, value_cotangents, preferred_element_type=F32)
    mixed = mixed_cube.reshape(seq_count, local_len, width)
    gated = (gates.astype(F32) * mixed.astype(F32)).astype(BF16)
    out_part = jnp.einsum("yrz,yrj->zj", gated, cotangent, preferred_element_type=F32)
    gate_cotangents = (back_gated.astype(F32) * mixed.astype(F32)).astype(BF16)
    gate_part = jnp.einsum("yrz,yrj->zj", inputs, gate_cotangents, preferred_element_type=F32)
    grad_inputs = (
        channel_back(value_cotangents, value_weight) + channel_back(gate_cotangents, gate_weight)
    ).astype(BF16)

    lanes = 128
    five = jnp.stack([value_part, gate_part, out_part, right_part, left_part])
    five = five.reshape(5, dp_size, -1, lanes).swapaxes(0, 1)
    five_rows = five.shape[2]
    twist = twiddle_part.reshape(dp_size, -1, lanes)
    twist_len = twist.shape[1]
    packed = jnp.concatenate(
        [five.reshape(dp_size, 5 * five_rows, lanes), twist], axis=1
    ).astype(BF16)
    mine = scatter_sum(packed, "dp")
    five_mine = mine[: 5 * five_rows].reshape(5, seq_size, -1, lanes).swapaxes(0, 1)
    piece = five_mine.shape[2]
    arrived = lax.all_to_all(five_mine.astype(BF16), "seq", split_axis=0, concat_axis=0, tiled=True)
    summed = jnp.sum(arrived.astype(F32), axis=0)
    tail = jnp.concatenate(
        [summed[3:].reshape(2 * piece, lanes), mine[5 * five_rows :]], axis=0
    )
    tail = exchange_sum(tail, "chan", chan_size)
    twist_sum = tail[2 * piece :].astype(BF16)
    done = jnp.concatenate([summed[:3], tail[: 2 * piece].reshape(2, piece, lanes)]).astype(BF16)
    spread = jnp.broadcast_to(done[None], (seq_size,) + done.shape)
    whole = lax.all_to_all(spread, "seq", split_axis=0, concat_axis=0, tiled=True)
    whole = whole.swapaxes(0, 1).reshape(5 * five_rows, lanes)
    final = gather(jnp.concatenate([whole, twist_sum], axis=0), "dp", dp_size).astype(F32)
    grads = final[:, : 5 * five_rows].reshape(dp_size, 5, five_rows, lanes).swapaxes(0, 1)
    grads = grads.reshape(5, width, -1)
    twiddle_sum = final[:, 5 * five_rows :].reshape(twiddle.shape)
    return (
        grad_inputs,
        grads[0][None],
        grads[1][None],
        grads[2][None],
        grads[3],
        grads[4],
        twiddle_sum,
    )


def solution(mesh):
    sizes = tuple(mesh.shape[name] for name in ("seq", "chan", "dp"))

    def body(*args):
        return on_device(sizes, *args)

    return jax.shard_map(
        body,
        mesh=mesh,
        in_specs=(
            P("dp", "seq", "chan"),
            P("chan", None, None),
            P("chan", None, None),
            P("chan", None, None),
            P(),
            P(),
            P("seq", None),
            P("dp", "seq", "chan"),
        ),
        out_specs=(
            P("dp", "seq", "chan"),
            P("chan", None, None),
            P("chan", None, None),
            P("chan", None, None),
            P(),
            P(),
            P("seq", None),
        ),
        check_vma=False,
    )
```

time: 1910 us -> 269 us (0.14)
  waiting for transfers between devices: 1720 us -> 77.1 us
  blocking collectives: 119 us -> 68.4 us
  starting transfers between devices: 10.6 us -> 60.1 us
    psum x2 -> x0, waiting for transfers between devices: 1670 us -> none  [the longest x1 1210 us: on_device(): lax.psum((value_block_weight, gate_block_weight, output_block_weight), ('...]
    psum x1 -> x0, blocking collectives: 50.5 us -> none  [on_device(): twiddle_sum = lax.psum(twiddle_part, ('chan', 'dp'))]
    ppermute x0 -> x9, starting transfers between devices: none -> 38 us  [swap(): return lax.ppermute(array, axis, [(i, i ^ step) for i in range(size)])]
  transfers between devices with their start and end apart: 4 -> 13, of which waited for: 4 -> 10; matrix products, arithmetic and copies ran while one was open for 1% -> 6% of each run, Pallas kernels for 0% -> 0%
where the time goes in v1:
time: 269 us; the launch traced here: 267 us
  waiting for transfers between devices  77.1 us (29%)
  blocking collectives  68.4 us (25%)
  starting transfers between devices  60.1 us (22%)
  local copies, waits for them, and re-layouts  29.8 us (11%)
  matrix products  23.7 us (9%)
  other arithmetic  6.85 us (3%)
    ppermute x9, starting transfers between devices, swap(): return lax.ppermute(array, axis, [(i, i ^ step) for i in range(size)])  38 us
    all_to_all x1, blocking collectives, on_device(): lax.all_to_all(back_cube, 'seq', split_axis=2, concat_axis=1, tiled=True)  36.6 us
    all_to_all x1, blocking collectives, on_device(): lax.all_to_all(twisted, 'seq', split_axis=2, concat_axis=1, tiled=True)  31.8 us
    all_to_all x1, waiting for transfers between devices, on_device(): lax.all_to_all(back_twist_cols, 'seq', split_axis=1, concat_axis=2, tiled...  25.1 us
    all_to_all x1, waiting for transfers between devices, on_device(): lax.all_to_all(mixed_cols, 'seq', split_axis=1, concat_axis=2, tiled=True)  18.9 us
    ppermute x9, waiting for transfers between devices, swap(): return lax.ppermute(array, axis, [(i, i ^ step) for i in range(size)])  17.6 us
    all_to_all x1, waiting for transfers between devices, on_device(): lax.all_to_all(five_mine.astype(BF16), 'seq', split_axis=0, concat_axis=0...  9.1 us
    dot_general x3, matrix products, channel_back(): return jnp.einsum('bxj,rj->bxr', rows, weight, preferred_element_type=F32)  7.55 us
  transfers between devices with their start and end apart: 13, of which 10 were waited for; matrix products, arithmetic and copies ran while one was open for 6% of the time, Pallas kernels for 0%

profile of v1, /device:TPU:1, one launch (start us, length us, event | category | flops | bytes accessed | tf_op | source)
XLA Modules:
  0.0 267.1 jit_solution(15156866169571552461)
XLA Ops:
  0.7 1.8 convolution_convert_fusion.2
  2.5 1.4 fusion.3
  4.5 36.6 %all_to_all.58 = bf16[1,8,256,256]{3,1,0,2:T(8,128)(2,1)S(1)} all-to-all(bf16[1,8,256,256]{3,1,0,2:T(8,128)(2,1)S(1)} %copy.111), channel_id=1, replica_groups=mesh['seq'=32,'chan'=4,'dp'=4] {'seq'}, dimensions={2} | all-to-all | bytes 2097152 | tf_op jit(solution)/shard_map/all_to_all | solution.py:70
  42.9 1.8 copy.115
  44.8 5.2 %all-to-all-start.1 = ((bf16[1,256,8,256]{3,2,0,1:T(8,128)(2,1)}), bf16[1,256,8,256]{3,2,0,1:T(8,128)(2,1)S(1)}, u32[]{:S(2)}, u32[]{:S(2)}) async-start(bf16[1,256,8,256]{3,2,0,1:T(8,128)(2,1)} %copy.115), calls=%async_computation.1 | async-start | bytes 2097152 | tf_op jit(solution)/shard_map/all_to_all | solution.py:78
  50.0 1.4 convolution_convert_fusion
  51.4 25.1 %all-to-all-done.1 = bf16[1,256,8,256]{3,2,0,1:T(8,128)(2,1)S(1)} async-done(((bf16[1,256,8,256]{3,2,0,1:T(8,128)(2,1)}), bf16[1,256,8,256]{3,2,0,1:T(8,128)(2,1)S(1)}, u32[]{:S(2)}, u32[]{:S(2)}) %all-to-all-start.1) | async-done | bytes 1048608 | tf_op jit(solution)/shard_map/all_to_all | solution.py:78
  76.6 1.7 copy_bitcast_fusion
  78.2 2.9 %copy.133 = f32[1,8,256,256]{2,3,1,0:T(8,128)} copy(f32[1,8,256,256]{3,2,1,0:T(8,128)} %copy_bitcast_fusion) | data formatting | bytes 4194304 | tf_op jit(solution)/shard_map/convert_element_type | solution.py:82
  81.2 2.4 fusion.6
  83.6 1.8 copy.120
  85.4 31.8 %all_to_all.59 = bf16[1,8,256,256]{3,1,0,2:T(8,128)(2,1)S(1)} all-to-all(bf16[1,8,256,256]{3,1,0,2:T(8,128)(2,1)} %copy.120), channel_id=1, replica_groups=mesh['seq'=32,'chan'=4,'dp'=4] {'seq'}, dimensions={2} | all-to-all | bytes 2097152 | tf_op jit(solution)/shard_map/all_to_all | solution.py:76
  117.6 1.5 fusion.9
  119.1 2.6 copy.124
  121.7 5.3 %all-to-all-start.3 = ((bf16[1,256,8,256]{3,2,0,1:T(8,128)(2,1)}), bf16[1,256,8,256]{3,2,0,1:T(8,128)(2,1)}, u32[]{:S(2)}, u32[]{:S(2)}) async-start(bf16[1,256,8,256]{3,2,0,1:T(8,128)(2,1)} %copy.124), calls=%async_computation.3 | async-start | bytes 2097152 | tf_op jit(solution)/shard_map/all_to_all | solution.py:80
  127.0 2.0 convolution_convert_fusion.4
  129.7 2.0 fusion.10
  132.5 2.2 fusion.11
  134.7 18.9 %all-to-all-done.3 = bf16[1,256,8,256]{3,2,0,1:T(8,128)(2,1)} async-done(((bf16[1,256,8,256]{3,2,0,1:T(8,128)(2,1)}), bf16[1,256,8,256]{3,2,0,1:T(8,128)(2,1)}, u32[]{:S(2)}, u32[]{:S(2)}) %all-to-all-start.3) | async-done | bytes 1048608 | tf_op jit(solution)/shard_map/all_to_all | solution.py:80
  153.6 1.5 convert_bitcast_fusion
  156.3 1.5 fusion.4
  159.1 1.6 stack.19
  160.7 1.7 convolution_convert_fusion.6
  162.4 1.6 constant_dynamic-update-slice_fusion.3
  166.0 1.1 copy.131
  167.2 3.1 %collective-permute-start = (bf16[644,128]{1,0:T(8,128)(2,1)S(1)}, bf16[644,128]{1,0:T(8,128)(2,1)S(1)}, u32[]{:S(2)}, u32[]{:S(2)}) collective-permute-start(bf16[644,128]{1,0:T(8,128)(2,1)S(1)} %get-tuple-element.16), channel_id=1, source_target_pairs={{0,1},{1,0},{2,3},{3,2},{4,5},{5,4},{6,7},{7,6},{8,9},{9,8},{10,11... | collective-permute-start | bytes 494600 | tf_op jit(solution)/shard_map/ppermute | solution.py:31
  170.3 4.5 %collective-permute-start.1 = (bf16[644,128]{1,0:T(8,128)(2,1)S(1)}, bf16[644,128]{1,0:T(8,128)(2,1)}, u32[]{:S(2)}, u32[]{:S(2)}) collective-permute-start(bf16[644,128]{1,0:T(8,128)(2,1)S(1)} %get-tuple-element.17), channel_id=1, source_target_pairs={{0,2},{1,3},{2,0},{3,1},{4,6},{5,7},{6,4},{7,5},{8,10},{9,11},{10,... | collective-permute-start | bytes 494600 | tf_op jit(solution)/shard_map/ppermute | solution.py:31
  174.8 2.1 collective-permute-start.2
  177.0 3.9 %collective-permute-done.1 = bf16[644,128]{1,0:T(8,128)(2,1)} collective-permute-done((bf16[644,128]{1,0:T(8,128)(2,1)S(1)}, bf16[644,128]{1,0:T(8,128)(2,1)}, u32[]{:S(2)}, u32[]{:S(2)}) %collective-permute-start.1) | collective-permute-done | bytes 164896 | tf_op jit(solution)/shard_map/ppermute | solution.py:31
  180.9 3.3 %collective-permute-done.2 = bf16[644,128]{1,0:T(8,128)(2,1)} collective-permute-done((bf16[644,128]{1,0:T(8,128)(2,1)S(1)}, bf16[644,128]{1,0:T(8,128)(2,1)}, u32[]{:S(2)}, u32[]{:S(2)}) %collective-permute-start.2) | collective-permute-done | bytes 164896 | tf_op jit(solution)/shard_map/ppermute | solution.py:31
  184.2 1.2 fusion.25
  186.2 5.7 %all-to-all-start.4 = ((bf16[32,5,4,128]{3,2,1,0:T(4,128)(2,1)}), bf16[32,5,4,128]{3,2,1,0:T(4,128)(2,1)}, u32[]{:S(2)}, u32[]{:S(2)}) async-start(bf16[32,5,4,128]{3,2,1,0:T(4,128)(2,1)} %bitcast.202), calls=%async_computation.4 | async-start | bytes 327680 | tf_op jit(solution)/shard_map/all_to_all | solution.py:112
  191.9 9.1 %all-to-all-done.4 = bf16[32,5,4,128]{3,2,1,0:T(4,128)(2,1)} async-done(((bf16[32,5,4,128]{3,2,1,0:T(4,128)(2,1)}), bf16[32,5,4,128]{3,2,1,0:T(4,128)(2,1)}, u32[]{:S(2)}, u32[]{:S(2)}) %all-to-all-start.4) | async-done | bytes 163872 | tf_op jit(solution)/shard_map/all_to_all | solution.py:112
  202.0 8.8 %collective-permute-start.3 = (f32[12,128]{1,0:T(8,128)S(1)}, f32[12,128]{1,0:T(8,128)S(1)}, u32[]{:S(2)}, u32[]{:S(2)}) collective-permute-start(f32[12,128]{1,0:T(8,128)S(1)} %pad_maximum_fusion.1), channel_id=1, source_target_pairs={{0,4},{4,0},{8,12},{12,8},{1,5},{5,1},{9,13},{13,9},{2,6},{6,2},{1... | collective-permute-start | bytes 18440 | tf_op jit(solution)/shard_map/ppermute | solution.py:31
  210.9 7.9 %collective-permute-start.4 = (f32[12,128]{1,0:T(8,128)S(1)}, f32[12,128]{1,0:T(8,128)S(1)}, u32[]{:S(2)}, u32[]{:S(2)}) collective-permute-start(f32[12,128]{1,0:T(8,128)S(1)} %pad_maximum_fusion.1), channel_id=1, source_target_pairs={{0,8},{4,12},{8,0},{12,4},{1,9},{5,13},{9,1},{13,5},{2,10},{6,14},... | collective-permute-start | bytes 18440 | tf_op jit(solution)/shard_map/ppermute | solution.py:31
  218.8 1.9 collective-permute-start.5
  220.7 3.2 %collective-permute-done.4 = f32[12,128]{1,0:T(8,128)S(1)} collective-permute-done((f32[12,128]{1,0:T(8,128)S(1)}, f32[12,128]{1,0:T(8,128)S(1)}, u32[]{:S(2)}, u32[]{:S(2)}) %collective-permute-start.4) | collective-permute-done | bytes 6176 | tf_op jit(solution)/shard_map/ppermute | solution.py:31
  224.0 3.1 %collective-permute-done.5 = f32[12,128]{1,0:T(8,128)S(1)} collective-permute-done((f32[12,128]{1,0:T(8,128)S(1)}, f32[12,128]{1,0:T(8,128)S(1)}, u32[]{:S(2)}, u32[]{:S(2)}) %collective-permute-start.5) | collective-permute-done | bytes 6176 | tf_op jit(solution)/shard_map/ppermute | solution.py:31
  227.8 5.8 %all-to-all-start.5 = ((bf16[32,5,4,128]{3,2,1,0:T(4,128)(2,1)}), bf16[32,5,4,128]{3,2,1,0:T(4,128)(2,1)S(1)}, u32[]{:S(2)}, u32[]{:S(2)}) async-start(bf16[32,5,4,128]{3,2,1,0:T(4,128)(2,1)} %broadcast_in_dim.24), calls=%async_computation.5 | async-start | bytes 327680 | tf_op jit(solution)/shard_map/all_to_all | solution.py:121
  233.7 2.7 %fusion.37 = f32[2048,256]{1,0:T(8,128)} fusion(bf16[2048,256]{1,0:T(8,128)(2,1)S(1)} %bitcast.185, bf16[1,256,256]{2,1,0:T(8,128)(2,1)} %param.9), kind=kOutput, calls=%fused_computation.75 | convolution fusion | flops 268435456 | bytes 3276800 | tf_op jit(solution)/shard_map/bxj,rj->bxr/dot_general | solution.py:15
  236.4 6.3 %all-to-all-done.5 = bf16[32,5,4,128]{3,2,1,0:T(4,128)(2,1)S(1)} async-done(((bf16[32,5,4,128]{3,2,1,0:T(4,128)(2,1)}), bf16[32,5,4,128]{3,2,1,0:T(4,128)(2,1)S(1)}, u32[]{:S(2)}, u32[]{:S(2)}) %all-to-all-start.5) | async-done | bytes 163872 | tf_op jit(solution)/shard_map/all_to_all | solution.py:121
  242.8 1.9 collective-permute-start.6
  244.8 3.0 %fusion.1 = bf16[1,2048,256]{2,1,0:T(8,128)(2,1)} fusion(f32[2048,256]{1,0:T(8,128)} %fusion.37, bf16[2048,256]{1,0:T(8,128)(2,1)S(1)} %get-tuple-element.10, bf16[1,256,256]{2,1,0:T(8,128)(2,1)S(1)} %copy-done.10), kind=kOutput, calls=%fused_computation.8 | convolution fusion | flops 269484032 | bytes 4325376 | tf_op jit(solution)/shard_map/bxj,rj->bxr/dot_general | solution.py:15
  247.8 3.9 %collective-permute-start.7 = (bf16[644,128]{1,0:T(8,128)(2,1)S(1)}, bf16[644,128]{1,0:T(8,128)(2,1)S(1)}, u32[]{:S(2)}, u32[]{:S(2)}) collective-permute-start(bf16[644,128]{1,0:T(8,128)(2,1)S(1)} %pad_maximum_fusion), channel_id=1, source_target_pairs={{0,2},{1,3},{2,0},{3,1},{4,6},{5,7},{6,4},{7,5},{8,10},{9,11},{10,... | collective-permute-start | bytes 494600 | tf_op jit(solution)/shard_map/ppermute | solution.py:31
  251.8 3.7 %collective-permute-start.8 = (bf16[644,128]{1,0:T(8,128)(2,1)S(1)}, bf16[644,128]{1,0:T(8,128)(2,1)S(1)}, u32[]{:S(2)}, u32[]{:S(2)}) collective-permute-start(bf16[644,128]{1,0:T(8,128)(2,1)S(1)} %pad_maximum_fusion), channel_id=1, source_target_pairs={{0,3},{1,2},{2,1},{3,0},{4,7},{5,6},{6,5},{7,4},{8,11},{9,10},{10,... | collective-permute-start | bytes 494600 | tf_op jit(solution)/shard_map/ppermute | solution.py:31
  256.4 3.2 %collective-permute-done.8 = bf16[644,128]{1,0:T(8,128)(2,1)S(1)} collective-permute-done((bf16[644,128]{1,0:T(8,128)(2,1)S(1)}, bf16[644,128]{1,0:T(8,128)(2,1)S(1)}, u32[]{:S(2)}, u32[]{:S(2)}) %collective-permute-start.8) | collective-permute-done | bytes 164896 | tf_op jit(solution)/shard_map/ppermute | solution.py:31
  260.7 1.7 slice.62
  262.4 1.7 slice.64
  (81 shorter events, 16.2 us)
Async XLA Ops:
  0.6 1.8 copy-start
  0.6 1.8 copy-start.9
  41.0 1.4 copy-start.12
  41.4 1.0 copy-start.7
  42.9 7.1 %copy-start.8 = (bf16[1,256,256]{2,1,0:T(8,128)(2,1)S(1)}, bf16[1,256,256]{2,1,0:T(8,128)(2,1)}, u32[]{:S(2)}) copy-start(bf16[1,256,256]{2,1,0:T(8,128)(2,1)} %param.9) | copy-start | bytes 393220
  44.8 31.8 %all-to-all-start.1 = ((bf16[1,256,8,256]{3,2,0,1:T(8,128)(2,1)}), bf16[1,256,8,256]{3,2,0,1:T(8,128)(2,1)S(1)}, u32[]{:S(2)}, u32[]{:S(2)}) async-start(bf16[1,256,8,256]{3,2,0,1:T(8,128)(2,1)} %copy.115), calls=%async_computation.1 | async-start | bytes 2097152 | tf_op jit(solution)/shard_map/all_to_all | solution.py:78
  76.6 4.6 %copy-start.3 = (bf16[1,256,8,256]{3,2,0,1:T(8,128)(2,1)}, bf16[1,256,8,256]{3,2,0,1:T(8,128)(2,1)S(1)}, u32[]{:S(2)}) copy-start(bf16[1,256,8,256]{3,2,0,1:T(8,128)(2,1)S(1)} %all-to-all-done.1) | copy-start | bytes 3145732
  78.2 2.9 %copy-start.13 = (bf16[256,256]{1,0:T(8,128)(2,1)S(1)}, bf16[256,256]{1,0:T(8,128)(2,1)}, u32[]{:S(2)}) copy-start(bf16[256,256]{1,0:T(8,128)(2,1)} %param.12) | copy-start | bytes 393220
  78.2 2.9 %copy-start.14 = (f32[8,256]{1,0:T(8,128)S(1)}, f32[8,256]{1,0:T(8,128)}, u32[]{:S(2)}) copy-start(f32[8,256]{1,0:T(8,128)} %param.14) | copy-start | bytes 24580
  117.5 4.2 %copy-start.5 = (bf16[1,32,8,8,256]{4,3,2,1,0:T(8,128)(2,1)}, bf16[1,32,8,8,256]{4,3,2,1,0:T(8,128)(2,1)S(1)}, u32[]{:S(2)}) copy-start(bf16[1,32,8,8,256]{4,3,2,1,0:T(8,128)(2,1)S(1)} %copy.122) | copy-start | bytes 3145732
  121.7 31.9 %all-to-all-start.3 = ((bf16[1,256,8,256]{3,2,0,1:T(8,128)(2,1)}), bf16[1,256,8,256]{3,2,0,1:T(8,128)(2,1)}, u32[]{:S(2)}, u32[]{:S(2)}) async-start(bf16[1,256,8,256]{3,2,0,1:T(8,128)(2,1)} %copy.124), calls=%async_computation.3 | async-start | bytes 2097152 | tf_op jit(solution)/shard_map/all_to_all | solution.py:80
  129.0 2.7 %copy-start.1 = (bf16[8,256,256]{1,2,0:T(8,128)(2,1)}, bf16[8,256,256]{1,2,0:T(8,128)(2,1)S(1)}, u32[]{:S(2)}) copy-start(bf16[8,256,256]{1,2,0:T(8,128)(2,1)S(1)} %convolution_convert_fusion.4) | copy-start | bytes 3145732
  155.1 1.2 copy-start.6
  157.8 2.9 %copy-start.4 = (bf16[1,2048,256]{2,1,0:T(8,128)(2,1)S(1)}, bf16[1,2048,256]{2,1,0:T(8,128)(2,1)}, u32[]{:S(2)}) copy-start(bf16[1,2048,256]{2,1,0:T(8,128)(2,1)} %param.15) | copy-start | bytes 3145732
  167.2 9.8 %collective-permute-start = (bf16[644,128]{1,0:T(8,128)(2,1)S(1)}, bf16[644,128]{1,0:T(8,128)(2,1)S(1)}, u32[]{:S(2)}, u32[]{:S(2)}) collective-permute-start(bf16[644,128]{1,0:T(8,128)(2,1)S(1)} %get-tuple-element.16), channel_id=1, source_target_pairs={{0,1},{1,0},{2,3},{3,2},{4,5},{5,4},{6,7},{7,6},{8,9},{9,8},{10,11... | collective-permute-start | bytes 494600 | tf_op jit(solution)/shard_map/ppermute | solution.py:31
  170.3 10.6 %collective-permute-start.1 = (bf16[644,128]{1,0:T(8,128)(2,1)S(1)}, bf16[644,128]{1,0:T(8,128)(2,1)}, u32[]{:S(2)}, u32[]{:S(2)}) collective-permute-start(bf16[644,128]{1,0:T(8,128)(2,1)S(1)} %get-tuple-element.17), channel_id=1, source_target_pairs={{0,2},{1,3},{2,0},{3,1},{4,6},{5,7},{6,4},{7,5},{8,10},{9,11},{10,... | collective-permute-start | bytes 494600 | tf_op jit(solution)/shard_map/ppermute | solution.py:31
  174.8 9.4 %collective-permute-start.2 = (bf16[644,128]{1,0:T(8,128)(2,1)S(1)}, bf16[644,128]{1,0:T(8,128)(2,1)}, u32[]{:S(2)}, u32[]{:S(2)}) collective-permute-start(bf16[644,128]{1,0:T(8,128)(2,1)S(1)} %get-tuple-element.18), channel_id=1, source_target_pairs={{0,3},{1,2},{2,1},{3,0},{4,7},{5,6},{6,5},{7,4},{8,11},{9,10},{10,... | collective-permute-start | bytes 494600 | tf_op jit(solution)/shard_map/ppermute | solution.py:31
  177.0 3.9 %copy-start.11 = (bf16[644,128]{1,0:T(8,128)(2,1)}, bf16[644,128]{1,0:T(8,128)(2,1)S(1)}, u32[]{:S(2)}) copy-start(bf16[644,128]{1,0:T(8,128)(2,1)S(1)} %collective-permute-done) | copy-start | bytes 494596
  185.4 48.3 %copy-start.2 = (bf16[8,256,256]{1,2,0:T(8,128)(2,1)S(1)}, bf16[8,256,256]{1,2,0:T(8,128)(2,1)}, u32[]{:S(2)}) copy-start(bf16[8,256,256]{1,2,0:T(8,128)(2,1)} %copy-done.1) | copy-start | bytes 3145732
  186.2 14.8 %all-to-all-start.4 = ((bf16[32,5,4,128]{3,2,1,0:T(4,128)(2,1)}), bf16[32,5,4,128]{3,2,1,0:T(4,128)(2,1)}, u32[]{:S(2)}, u32[]{:S(2)}) async-start(bf16[32,5,4,128]{3,2,1,0:T(4,128)(2,1)} %bitcast.202), calls=%async_computation.4 | async-start | bytes 327680 | tf_op jit(solution)/shard_map/all_to_all | solution.py:112
  202.0 18.7 %collective-permute-start.3 = (f32[12,128]{1,0:T(8,128)S(1)}, f32[12,128]{1,0:T(8,128)S(1)}, u32[]{:S(2)}, u32[]{:S(2)}) collective-permute-start(f32[12,128]{1,0:T(8,128)S(1)} %pad_maximum_fusion.1), channel_id=1, source_target_pairs={{0,4},{4,0},{8,12},{12,8},{1,5},{5,1},{9,13},{13,9},{2,6},{6,2},{1... | collective-permute-start | bytes 18440 | tf_op jit(solution)/shard_map/ppermute | solution.py:31
  210.9 13.1 %collective-permute-start.4 = (f32[12,128]{1,0:T(8,128)S(1)}, f32[12,128]{1,0:T(8,128)S(1)}, u32[]{:S(2)}, u32[]{:S(2)}) collective-permute-start(f32[12,128]{1,0:T(8,128)S(1)} %pad_maximum_fusion.1), channel_id=1, source_target_pairs={{0,8},{4,12},{8,0},{12,4},{1,9},{5,13},{9,1},{13,5},{2,10},{6,14},... | collective-permute-start | bytes 18440 | tf_op jit(solution)/shard_map/ppermute | solution.py:31
  218.8 8.3 %collective-permute-start.5 = (f32[12,128]{1,0:T(8,128)S(1)}, f32[12,128]{1,0:T(8,128)S(1)}, u32[]{:S(2)}, u32[]{:S(2)}) collective-permute-start(f32[12,128]{1,0:T(8,128)S(1)} %pad_maximum_fusion.1), channel_id=1, source_target_pairs={{0,12},{4,8},{8,4},{12,0},{1,13},{5,9},{9,5},{13,1},{2,14},{6,10},... | collective-permute-start | bytes 18440 | tf_op jit(solution)/shard_map/ppermute | solution.py:31
  227.8 16.9 %copy-start.10 = (bf16[1,256,256]{2,1,0:T(8,128)(2,1)S(1)}, bf16[1,256,256]{2,1,0:T(8,128)(2,1)}, u32[]{:S(2)}) copy-start(bf16[1,256,256]{2,1,0:T(8,128)(2,1)} %param.10) | copy-start | bytes 393220
  227.8 14.9 %all-to-all-start.5 = ((bf16[32,5,4,128]{3,2,1,0:T(4,128)(2,1)}), bf16[32,5,4,128]{3,2,1,0:T(4,128)(2,1)S(1)}, u32[]{:S(2)}, u32[]{:S(2)}) async-start(bf16[32,5,4,128]{3,2,1,0:T(4,128)(2,1)} %broadcast_in_dim.24), calls=%async_computation.5 | async-start | bytes 327680 | tf_op jit(solution)/shard_map/all_to_all | solution.py:121
  242.8 12.8 %collective-permute-start.6 = (bf16[644,128]{1,0:T(8,128)(2,1)S(1)}, bf16[644,128]{1,0:T(8,128)(2,1)S(1)}, u32[]{:S(2)}, u32[]{:S(2)}) collective-permute-start(bf16[644,128]{1,0:T(8,128)(2,1)S(1)} %pad_maximum_fusion), channel_id=1, source_target_pairs={{0,1},{1,0},{2,3},{3,2},{4,5},{5,4},{6,7},{7,6},{8,9},{9,8},{10,11... | collective-permute-start | bytes 494600 | tf_op jit(solution)/shard_map/ppermute | solution.py:31
  247.8 8.6 %collective-permute-start.7 = (bf16[644,128]{1,0:T(8,128)(2,1)S(1)}, bf16[644,128]{1,0:T(8,128)(2,1)S(1)}, u32[]{:S(2)}, u32[]{:S(2)}) collective-permute-start(bf16[644,128]{1,0:T(8,128)(2,1)S(1)} %pad_maximum_fusion), channel_id=1, source_target_pairs={{0,2},{1,3},{2,0},{3,1},{4,6},{5,7},{6,4},{7,5},{8,10},{9,11},{10,... | collective-permute-start | bytes 494600 | tf_op jit(solution)/shard_map/ppermute | solution.py:31
  251.8 7.9 %collective-permute-start.8 = (bf16[644,128]{1,0:T(8,128)(2,1)S(1)}, bf16[644,128]{1,0:T(8,128)(2,1)S(1)}, u32[]{:S(2)}, u32[]{:S(2)}) collective-permute-start(bf16[644,128]{1,0:T(8,128)(2,1)S(1)} %pad_maximum_fusion), channel_id=1, source_target_pairs={{0,3},{1,2},{2,1},{3,0},{4,7},{5,6},{6,5},{7,4},{8,11},{9,10},{10,... | collective-permute-start | bytes 494600 | tf_op jit(solution)/shard_map/ppermute | solution.py:31

commit v2 on v0

v2 whole, which is shorter than its diff:
```python
import functools

import jax
import jax.numpy as jnp
from jax import lax
from jax.experimental import pallas as pl
from jax.experimental.pallas import tpu as pltpu
from jax.sharding import PartitionSpec as P

F32 = jnp.float32
BF16 = jnp.bfloat16
LANES = 128
VMEM = pl.BlockSpec(memory_space=pltpu.VMEM)
PARAMS = pltpu.CompilerParams(vmem_limit_bytes=50 * 1024 * 1024)


def dot(a, b, dims=((1,), (0,))):
    return lax.dot_general(a, b, (dims, ((), ())), preferred_element_type=F32)


NT = ((1,), (1,))
TN = ((0,), (0,))


def put_wide(ref, value):
    for h in range(ref.shape[0]):
        ref[h] = value[:, h * LANES : (h + 1) * LANES]


def get_wide(ref):
    return jnp.concatenate([ref[h] for h in range(ref.shape[0])], axis=1)


def every(ref, start, count, step, halves=range(2)):
    return jnp.concatenate([ref[h, pl.ds(start, count, stride=step), :] for h in halves], axis=1)


def put_every(ref, start, count, step, value, first=0):
    for h in range(value.shape[1] // LANES):
        ref[first + h, pl.ds(start, count, stride=step), :] = value[:, h * LANES : (h + 1) * LANES]


def place_major(ref, groups, places, halves=range(2)):
    return jnp.concatenate([every(ref, p, groups, places, halves) for p in range(places)], axis=0)


def place_major_tables(right_ref, twiddle_ref, wide, groups, places):
    put_wide(wide, right_ref[...].astype(F32))
    right = place_major(wide, groups, places).astype(BF16)
    rows = twiddle_ref.shape[0]
    wide[0] = jnp.concatenate(
        [twiddle_ref[...], jnp.zeros((LANES - rows, twiddle_ref.shape[1]), F32)], axis=0
    ).T
    twist = place_major(wide, groups, places, range(1))
    return right, twist


def rows_before(
    groups, x_ref, ct_ref, wv_ref, wg_ref, wo_ref, right_ref, twiddle_ref,
    send_ref, value_ref, gate_ref, back_ref, wide, cols,
):
    blocks = twiddle_ref.shape[0]
    size = right_ref.shape[0]
    places = size // groups
    right, twist = place_major_tables(right_ref, twiddle_ref, wide, groups, places)
    for i in range(blocks):
        rows = slice(i * size, (i + 1) * size)
        x = x_ref[rows, :]
        gates = dot(x, wg_ref[...]).astype(BF16)
        back = dot(ct_ref[rows, :], wo_ref[...], NT).astype(BF16)
        values = dot(x, wv_ref[...]).astype(BF16)
        gate_ref[rows, :] = gates
        back_ref[rows, :] = back
        value_ref[rows, :] = values
        put_wide(wide, back.astype(F32) * gates.astype(F32))
        twisted = dot(right, values) * twist[:, i : i + 1]
        for p in range(places):
            put_every(cols, i, groups, blocks, every(wide, p, groups, places), 2 * p)
            part = twisted[p * groups : (p + 1) * groups]
            put_every(cols, i, groups, blocks, part, 2 * (places + p))
    for t in range(4 * places):
        send_ref[:, t * LANES : (t + 1) * LANES] = cols[t].astype(BF16)


def columns(left_ref, cols_ref, send_ref, grad_ref):
    left = left_ref[...]
    half = cols_ref.shape[1] // 2
    step = 512
    for at in range(0, half, step):
        back = cols_ref[:, at : at + step]
        twist = cols_ref[:, half + at : half + at + step]
        send_ref[:, at : at + step] = dot(left, back, TN).astype(BF16)
        send_ref[:, half + at : half + at + step] = dot(left, twist).astype(BF16)
    grad_ref[...] = dot(cols_ref[:, :half], cols_ref[:, half:], NT)


def rows_after(
    groups, came_ref, x_ref, ct_ref, value_ref, gate_ref, back_ref, wv_ref, wg_ref,
    right_ref, twiddle_ref, left_grad_ref,
    gi_ref, low_ref, high_ref,
    wide, cols, gated_all, back_gates_all, back_values_all,
):
    blocks = twiddle_ref.shape[0]
    size = right_ref.shape[0]
    places = size // groups
    right, twist = place_major_tables(right_ref, twiddle_ref, wide, groups, places)
    for t in range(4 * places):
        cols[t] = came_ref[:, t * LANES : (t + 1) * LANES].astype(F32)
    lane = lax.broadcasted_iota(jnp.int32, (size, LANES), 1)
    right_grad = jnp.zeros((size, size), F32)
    twist_grad = jnp.zeros((size, LANES), F32)
    for i in range(blocks):
        rows = slice(i * size, (i + 1) * size)
        values = value_ref[rows, :]
        back = jnp.concatenate(
            [
                every(cols, i, groups, blocks, (2 * p, 2 * p + 1))
                for p in range(places)
            ],
            axis=0,
        )
        rotated = dot(right, values)
        column = jnp.sum(back * rotated, axis=1, keepdims=True)
        twist_grad = jnp.where(lane == i, column, twist_grad)
        back_rotated = (back * twist[:, i : i + 1]).astype(BF16)
        back_values = dot(right, back_rotated, TN).astype(BF16)
        right_grad += dot(back_rotated, values, NT)
        for p in range(places):
            at = 2 * (places + p)
            put_every(wide, p, groups, places, every(cols, i, groups, blocks, (at, at + 1)))
        mixed = get_wide(wide)
        back_gates = (back_ref[rows, :].astype(F32) * mixed).astype(BF16)
        gated_all[rows, :] = (gate_ref[rows, :].astype(F32) * mixed).astype(BF16)
        back_gates_all[rows, :] = back_gates
        back_values_all[rows, :] = back_values
        gi_ref[rows, :] = (
            dot(back_values, wv_ref[...], NT) + dot(back_gates, wg_ref[...], NT)
        ).astype(BF16)

    def put(ref, tile, grad):
        for h in range(2):
            ref[h * size : (h + 1) * size, tile * LANES : (tile + 1) * LANES] = grad[
                :, h * LANES : (h + 1) * LANES
            ].astype(BF16)

    put(low_ref, 0, dot(x_ref[...], back_values_all[...], TN))
    put(high_ref, 0, dot(x_ref[...], back_gates_all[...], TN))
    put(low_ref, 1, dot(gated_all[...], ct_ref[...], TN))
    put(high_ref, 2, left_grad_ref[...])
    for p in range(places):
        put_every(wide, p, groups, places, right_grad[p * groups : (p + 1) * groups])
    put(low_ref, 2, get_wide(wide))
    for p in range(places):
        put_every(wide, p, groups, places, twist_grad[p * groups : (p + 1) * groups])
    flat = wide[0].T[:blocks]
    own = jnp.concatenate([flat[:, :LANES], flat[:, LANES:]], axis=0).astype(BF16)
    high_ref[:, LANES : 2 * LANES] = jnp.zeros((2 * size, LANES), BF16)
    at = pl.multiple_of(lax.axis_index("seq") * 2 * blocks, 2 * blocks)
    high_ref[pl.ds(at, 2 * blocks), LANES : 2 * LANES] = own


def unpack(mine_ref, other_ref, value_ref, gate_ref, out_ref, right_ref, left_ref, twiddle_ref):
    size = value_ref.shape[0]
    blocks = twiddle_ref.shape[0]
    seq = lax.axis_index("seq")

    def take(ref, source, tile):
        for h in range(2):
            ref[:, h * LANES : (h + 1) * LANES] = source[
                h * size : (h + 1) * size, tile * LANES : (tile + 1) * LANES
            ].astype(F32)

    def spread(low, high):
        take(value_ref, low, 0)
        take(out_ref, low, 1)
        take(right_ref, low, 2)
        take(gate_ref, high, 0)
        take(left_ref, high, 2)
        at = pl.multiple_of(seq * 2 * blocks, 2 * blocks)
        own = high[pl.ds(at, 2 * blocks), LANES : 2 * LANES].astype(F32)
        twiddle_ref[:, :LANES] = own[:blocks]
        twiddle_ref[:, LANES:] = own[blocks:]

    @pl.when(seq % 2 == 0)
    def _():
        spread(mine_ref, other_ref)

    @pl.when(seq % 2 == 1)
    def _():
        spread(other_ref, mine_ref)


def shape(*dims, dtype=BF16):
    return jax.ShapeDtypeStruct(dims, dtype)


def cost(flops, moved):
    return pl.CostEstimate(flops=int(flops), bytes_accessed=int(moved), transcendentals=0)


def on_device(sizes, inputs, w_value, w_gate, w_out, mon_right, mon_left, twiddle, cotangent):
    seq_size, chan_size, dp_size = sizes
    _, length, width = inputs.shape
    size = mon_right.shape[0]
    blocks = length // size
    places = size // seq_size
    x, ct = inputs[0], cotangent[0]
    cols = places * width
    square = 2 * length * width * width

    send, values, gates, back_gated = pl.pallas_call(
        functools.partial(rows_before, seq_size),
        out_shape=(shape(seq_size * blocks, 2 * cols),) + (shape(length, width),) * 3,
        in_specs=[VMEM] * 7,
        out_specs=(VMEM,) * 4,
        scratch_shapes=[
            pltpu.VMEM((2, size, LANES), F32),
            pltpu.VMEM((4 * places, seq_size * blocks, LANES), F32),
        ],
        compiler_params=PARAMS,
        cost_estimate=cost(4 * square, 14 * length * width),
        name="rows_before",
    )(x, ct, w_value[0], w_gate[0], w_out[0], mon_right, twiddle)
    came = lax.all_to_all(send, "seq", 0, 0, tiled=True)
    send_back, left_grad = pl.pallas_call(
        columns,
        out_shape=(shape(seq_size * blocks, 2 * cols), shape(size, size, dtype=F32)),
        in_specs=[VMEM] * 2,
        out_specs=(VMEM,) * 2,
        compiler_params=PARAMS,
        cost_estimate=cost(3 * square, 8 * length * width),
        name="columns",
    )(mon_left, came)
    came_back = lax.all_to_all(send_back, "seq", 0, 0, tiled=True)
    grad_inputs, low, high = pl.pallas_call(
        functools.partial(rows_after, seq_size),
        out_shape=(
            shape(length, width),
            shape(2 * size, 3 * LANES),
            shape(2 * size, 3 * LANES),
        ),
        in_specs=[VMEM] * 11,
        out_specs=(VMEM,) * 3,
        scratch_shapes=[
            pltpu.VMEM((2, size, LANES), F32),
            pltpu.VMEM((4 * places, seq_size * blocks, LANES), F32),
            pltpu.VMEM((length, width), BF16),
            pltpu.VMEM((length, width), BF16),
            pltpu.VMEM((length, width), BF16),
        ],
        compiler_params=PARAMS,
        cost_estimate=cost(8 * square, 16 * length * width),
        name="rows_after",
    )(
        came_back, x, ct, values, gates, back_gated,
        w_value[0], w_gate[0], mon_right, twiddle, left_grad,
    )

    even = lax.axis_index("seq") % 2 == 0
    swap = [(i, i ^ 1) for i in range(seq_size)]
    like = [
        [seq * dp_size + dp for seq in range(core, seq_size, 2) for dp in range(dp_size)]
        for core in range(2)
    ]
    peers = len(like[0])
    theirs = lax.ppermute(jnp.where(even, high, low), "seq", swap)
    pair = (jnp.where(even, low, high).astype(F32) + theirs.astype(F32)).astype(BF16)
    arrived = lax.all_to_all(pair, ("seq", "dp"), 0, 0, tiled=True, axis_index_groups=like)
    mine = jnp.sum(arrived.reshape(peers, -1, 3 * LANES).astype(F32), axis=0)
    factors = jnp.broadcast_to(mine[None, :, LANES:], (chan_size,) + mine[:, LANES:].shape)
    factors = jnp.sum(lax.all_to_all(factors, "chan", 0, 0, tiled=True), axis=0)
    middle = jnp.where(even, mine[:, LANES : 2 * LANES], factors[:, :LANES])
    done = jnp.concatenate([mine[:, :LANES], middle, factors[:, LANES:]], axis=1).astype(BF16)
    spread = jnp.broadcast_to(done[None], (peers,) + done.shape).reshape(pair.shape)
    half = lax.all_to_all(spread, ("seq", "dp"), 0, 0, tiled=True, axis_index_groups=like)
    other = lax.ppermute(half, "seq", swap)
    g_value, g_gate, g_out, g_right, g_left, g_twiddle = pl.pallas_call(
        unpack,
        out_shape=(shape(size, size, dtype=F32),) * 5 + (shape(blocks, size, dtype=F32),),
        in_specs=[VMEM] * 2,
        out_specs=(VMEM,) * 6,
        compiler_params=PARAMS,
        name="unpack",
    )(half, other)
    return grad_inputs[None], g_value[None], g_gate[None], g_out[None], g_right, g_left, g_twiddle


def solution(mesh):
    sizes = tuple(mesh.shape[name] for name in ("seq", "chan", "dp"))
    return jax.shard_map(
        functools.partial(on_device, sizes),
        mesh=mesh,
        in_specs=(
            P("dp", "seq", "chan"),
            P("chan", None, None),
            P("chan", None, None),
            P("chan", None, None),
            P(),
            P(),
            P("seq", None),
            P("dp", "seq", "chan"),
        ),
        out_specs=(
            P("dp", "seq", "chan"),
            P("chan", None, None),
            P("chan", None, None),
            P("chan", None, None),
            P(),
            P(),
            P("seq", None),
        ),
        check_vma=False,
    )
```

time: 1910 us -> 211 us (0.11)
  waiting for transfers between devices: 1720 us -> 50.8 us
  matrix products: 23.2 us -> 0 us
  local copies, waits for them, and re-layouts: 24 us -> 4.4 us
    psum x2 -> x0, waiting for transfers between devices: 1670 us -> none  [the longest x1 1210 us: on_device(): lax.psum((value_block_weight, gate_block_weight, output_block_weight), ('...]
    all_to_all x2 -> x4, blocking collectives: 68.4 us -> 122 us  [the longest x1 60.6 us: on_device(): came = lax.all_to_all(send, 'seq', 0, 0, tiled=True)]
    psum x1 -> x0, blocking collectives: 50.5 us -> none  [on_device(): twiddle_sum = lax.psum(twiddle_part, ('chan', 'dp'))]
    dot_general x14 -> x0, matrix products: 23.2 us -> none  [the longest x3 6.61 us: channel_back(): jnp.einsum('bxj,rj->bxr', input_activations, weight_matrix, preferred_ele...]
    all_to_all x2 -> x1, waiting for transfers between devices: 48.8 us -> 48.2 us  [on_device(): came_back = lax.all_to_all(send_back, 'seq', 0, 0, tiled=True)]
  transfers between devices with their start and end apart: 4 -> 3, of which waited for: 4 -> 3; matrix products, arithmetic and copies ran while one was open for 1% -> 0% of each run, Pallas kernels for 0% -> 0%
where the time goes in v2:
time: 211 us
  blocking collectives  122 us (58%)
  waiting for transfers between devices  50.8 us (24%)
  Pallas kernels  17.5 us (8%)
  starting transfers between devices  14.6 us (7%)
  local copies, waits for them, and re-layouts  4.4 us (2%)
    all_to_all x1, blocking collectives, on_device(): came = lax.all_to_all(send, 'seq', 0, 0, tiled=True)  60.6 us
    all_to_all x1, waiting for transfers between devices, on_device(): came_back = lax.all_to_all(send_back, 'seq', 0, 0, tiled=True)  48.2 us
    all_to_all x1, blocking collectives, on_device(): factors = jnp.sum(lax.all_to_all(factors, 'chan', 0, 0, tiled=True), axis=0)  23.8 us
    all_to_all x1, blocking collectives, on_device(): lax.all_to_all(pair, ('seq', 'dp'), 0, 0, tiled=True, axis_index_groups=l...  20.8 us
    all_to_all x1, blocking collectives, on_device(): lax.all_to_all(spread, ('seq', 'dp'), 0, 0, tiled=True, axis_index_groups...  17.3 us
    pallas_call x1, Pallas kernels, on_device(): pl.pallas_call(functools.partial(rows_after, seq_size), out_shape=(shape(...  6.83 us
    ppermute x1, starting transfers between devices, on_device(): other = lax.ppermute(half, 'seq', swap)  6.48 us
    pallas_call x1, Pallas kernels, on_device(): pl.pallas_call(functools.partial(rows_before, seq_size), out_shape=(shape...  5.55 us
  transfers between devices with their start and end apart: 3, of which 3 were waited for; matrix products, arithmetic and copies ran while one was open for 0% of the time, Pallas kernels for 0%

profile of v2, /device:TPU:1, one launch (start us, length us, event | category | flops | bytes accessed | tf_op | source)
XLA Modules:
  0.0 210.8 jit_solution(12671382937690909091)
XLA Ops:
  0.6 0.0 copy-start.5
  0.6 0.9 copy-done.5
  1.5 0.0 copy-start.7
  1.5 0.9 copy-done.7
  2.4 0.0 copy-start.9
  2.4 0.9 copy-done.9
  3.3 0.0 copy-start.11
  3.4 0.7 copy-done.11
  4.0 0.0 copy-start.13
  4.0 0.9 copy-done.13
  5.0 5.6 %rows_before.1 = (bf16[256,4096]{1,0:T(8,128)(2,1)}, bf16[2048,256]{1,0:T(8,128)(2,1)S(1)}, bf16[2048,256]{1,0:T(8,128)(2,1)S(1)}, bf16[2048,256]{1,0:T(8,128)(2,1)S(1)}) custom-call(bf16[2048,256]{1,0:T(8,128)(2,1)} %bitcast.18, bf16[2048,256]{1,0:T(8,128)(2,1)} %bitcast.20, bf16[256,256]{1,0:T(8,128)(2,1)S(1)} %bitcast.22, bf16[256,256]{1,0:T(8,128)(2,1)S(1)} %bitcast.24, ...), custom_call_target="tpu_custom_call" | custom-call | flops 1073741824 | bytes 7340032 | tf_op jit(solution)/shard_map/rows_before/pallas_call | solution.py:211
  10.5 0.0 copy-start.2
  10.5 0.0 copy-start.3
  10.5 0.0 copy-start.4
  10.5 0.0 copy-start.14
  10.5 60.6 %all_to_all.44 = bf16[32,8,4096]{2,1,0:T(8,128)(2,1)} all-to-all(bf16[32,8,4096]{2,1,0:T(8,128)(2,1)} %bitcast.27), channel_id=1, replica_groups=mesh['seq'=32,'chan'=4,'dp'=4] {'seq'}, dimensions={0} | all-to-all | bytes 4194304 | tf_op jit(solution)/shard_map/all_to_all | solution.py:224
  71.1 0.0 copy-done.2
  71.1 0.0 copy-done.3
  71.1 0.0 copy-done.4
  71.1 0.0 copy-done.14
  71.1 4.0 %columns.1 = (bf16[256,4096]{1,0:T(8,128)(2,1)}, f32[256,256]{1,0:T(8,128)S(1)}) custom-call(bf16[256,256]{1,0:T(8,128)(2,1)S(1)} %copy-done.14, bf16[256,4096]{1,0:T(8,128)(2,1)} %bitcast.28), custom_call_target="tpu_custom_call" | custom-call | flops 805306368 | bytes 4194304 | tf_op jit(solution)/shard_map/columns/pallas_call | solution.py:225
  75.1 0.0 copy-start
  75.1 0.0 copy-start.1
  75.1 0.0 copy-start.6
  75.1 0.0 copy-start.8
  75.1 0.0 copy-start.10
  75.1 0.0 copy-start.12
  75.1 5.3 %all-to-all-start.1 = ((bf16[32,8,4096]{2,1,0:T(8,128)(2,1)}), bf16[32,8,4096]{2,1,0:T(8,128)(2,1)}, u32[]{:S(2)}, u32[]{:S(2)}) async-start(bf16[32,8,4096]{2,1,0:T(8,128)(2,1)} %bitcast.7), calls=%async_computation.1 | async-start | bytes 4194304 | tf_op jit(solution)/shard_map/all_to_all | solution.py:234
  80.4 48.2 %all-to-all-done.1 = bf16[32,8,4096]{2,1,0:T(8,128)(2,1)} async-done(((bf16[32,8,4096]{2,1,0:T(8,128)(2,1)}), bf16[32,8,4096]{2,1,0:T(8,128)(2,1)}, u32[]{:S(2)}, u32[]{:S(2)}) %all-to-all-start.1) | async-done | bytes 2097184 | tf_op jit(solution)/shard_map/all_to_all | solution.py:234
  128.6 0.0 copy-done
  128.6 0.0 copy-done.1
  128.6 0.0 copy-done.6
  128.6 0.0 copy-done.8
  128.6 0.0 copy-done.10
  128.7 0.0 copy-done.12
  128.7 6.8 %rows_after.1 = (bf16[2048,256]{1,0:T(8,128)(2,1)}, bf16[512,384]{1,0:T(8,128)(2,1)S(1)}, bf16[512,384]{1,0:T(8,128)(2,1)S(1)}) custom-call(bf16[256,4096]{1,0:T(8,128)(2,1)} %bitcast.8.came_ref, bf16[2048,256]{1,0:T(8,128)(2,1)S(1)} %bitcast.19, bf16[2048,256]{1,0:T(8,128)(2,1)S(1)} %bitcast.21, bf16[2048,256]{1,0:T(8,128)(2,1)} %copy-done.2, ...), custom_call_target="tpu_custom_call" | custom-call | flops 2147483648 | bytes 8388608 | tf_op jit(solution)/shard_map/rows_after/pallas_call | solution.py:235
  135.5 2.8 %collective-permute-start = (bf16[512,384]{1,0:T(8,128)(2,1)S(1)}, bf16[512,384]{1,0:T(8,128)(2,1)S(1)}, u32[]{:S(2)}, u32[]{:S(2)}) collective-permute-start(bf16[512,384]{1,0:T(8,128)(2,1)S(1)} %broadcast_select_fusion), channel_id=1, source_target_pairs={{0,16},{16,0},{32,48},{48,32},{64,80},{80,64},{96,112},{112,96},{1... | collective-permute-start | bytes 1179656 | tf_op jit(solution)/shard_map/ppermute | solution.py:266
  138.3 1.3 collective-permute-done
  139.7 0.1 fusion
  139.8 20.8 %all_to_all.45 = bf16[64,8,384]{2,1,0:T(8,128)(2,1)S(1)} all-to-all(bf16[64,8,384]{2,1,0:T(8,128)(2,1)S(1)} %fusion), channel_id=1, replica_groups={{0,1,2,3,32,33,34,35,64,65,66,67,96,97,98,99,128,129,130,131,160,161,16..., dimensions={0} | all-to-all | bytes 786432 | tf_op jit(solution)/shard_map/all_to_all | solution.py:268
  160.6 0.1 convert_reduce_fusion
  160.7 23.8 %all_to_all.46 = f32[4,8,256]{2,1,0:T(8,128)S(1)} all-to-all(f32[4,8,256]{2,1,0:T(8,128)S(1)} %broadcast_in_dim.25), channel_id=1, replica_groups=mesh['seq'=32,'chan'=4,'dp'=4] {'chan'}, dimensions={0} | all-to-all | bytes 65536 | tf_op jit(solution)/shard_map/all_to_all | solution.py:271
  184.6 17.3 %all_to_all.47 = bf16[64,8,384]{2,1,0:T(8,128)(2,1)S(1)} all-to-all(bf16[64,8,384]{2,1,0:T(8,128)(2,1)S(1)} %broadcast_in_dim.26), channel_id=1, replica_groups={{0,1,2,3,32,33,34,35,64,65,66,67,96,97,98,99,128,129,130,131,160,161,16..., dimensions={0} | all-to-all | bytes 786432 | tf_op jit(solution)/shard_map/all_to_all | solution.py:275
  201.8 6.5 %collective-permute-start.1 = (bf16[512,384]{1,0:T(8,128)(2,1)S(1)}, bf16[512,384]{1,0:T(8,128)(2,1)S(1)}, u32[]{:S(2)}, u32[]{:S(2)}) collective-permute-start(bf16[512,384]{1,0:T(8,128)(2,1)S(1)} %bitcast.16), channel_id=1, source_target_pairs={{0,16},{16,0},{32,48},{48,32},{64,80},{80,64},{96,112},{112,96},{1... | collective-permute-start | bytes 1179656 | tf_op jit(solution)/shard_map/ppermute | solution.py:276
  208.3 1.3 collective-permute-done.1.other_ref
  209.7 1.1 unpack.1
  (7 shorter events, 0.1 us)
Async XLA Ops:
  0.6 0.9 copy-start.5
  1.5 0.9 copy-start.7
  2.4 0.9 copy-start.9
  3.3 0.7 copy-start.11
  4.0 0.9 copy-start.13
  10.5 60.6 %copy-start.2 = (bf16[2048,256]{1,0:T(8,128)(2,1)}, bf16[2048,256]{1,0:T(8,128)(2,1)S(1)}, u32[]{:S(2)}) copy-start(bf16[2048,256]{1,0:T(8,128)(2,1)S(1)} %get-tuple-element.24.value_ref) | copy-start | bytes 3145732
  10.5 60.6 %copy-start.3 = (bf16[2048,256]{1,0:T(8,128)(2,1)}, bf16[2048,256]{1,0:T(8,128)(2,1)S(1)}, u32[]{:S(2)}) copy-start(bf16[2048,256]{1,0:T(8,128)(2,1)S(1)} %get-tuple-element.25.gate_ref) | copy-start | bytes 3145732
  10.5 60.6 %copy-start.4 = (bf16[2048,256]{1,0:T(8,128)(2,1)}, bf16[2048,256]{1,0:T(8,128)(2,1)S(1)}, u32[]{:S(2)}) copy-start(bf16[2048,256]{1,0:T(8,128)(2,1)S(1)} %get-tuple-element.26.back_ref) | copy-start | bytes 3145732
  10.5 60.6 %copy-start.14 = (bf16[256,256]{1,0:T(8,128)(2,1)S(1)}, bf16[256,256]{1,0:T(8,128)(2,1)}, u32[]{:S(2)}) copy-start(bf16[256,256]{1,0:T(8,128)(2,1)} %left_ref.1) | copy-start | bytes 393220
  75.1 53.6 %copy-start = (bf16[1,2048,256]{2,1,0:T(8,128)(2,1)S(1)}, bf16[1,2048,256]{2,1,0:T(8,128)(2,1)}, u32[]{:S(2)}) copy-start(bf16[1,2048,256]{2,1,0:T(8,128)(2,1)} %param.8) | copy-start | bytes 3145732
  75.1 53.6 %copy-start.1 = (bf16[1,2048,256]{2,1,0:T(8,128)(2,1)S(1)}, bf16[1,2048,256]{2,1,0:T(8,128)(2,1)}, u32[]{:S(2)}) copy-start(bf16[1,2048,256]{2,1,0:T(8,128)(2,1)} %param.15) | copy-start | bytes 3145732
  75.1 53.6 %copy-start.6 = (bf16[1,256,256]{2,1,0:T(8,128)(2,1)S(1)}, bf16[1,256,256]{2,1,0:T(8,128)(2,1)}, u32[]{:S(2)}) copy-start(bf16[1,256,256]{2,1,0:T(8,128)(2,1)} %param.9) | copy-start | bytes 393220
  75.1 53.6 %copy-start.8 = (bf16[1,256,256]{2,1,0:T(8,128)(2,1)S(1)}, bf16[1,256,256]{2,1,0:T(8,128)(2,1)}, u32[]{:S(2)}) copy-start(bf16[1,256,256]{2,1,0:T(8,128)(2,1)} %param.10) | copy-start | bytes 393220
  75.1 53.6 %copy-start.10 = (bf16[256,256]{1,0:T(8,128)(2,1)S(1)}, bf16[256,256]{1,0:T(8,128)(2,1)}, u32[]{:S(2)}) copy-start(bf16[256,256]{1,0:T(8,128)(2,1)} %right_ref.3) | copy-start | bytes 393220
  75.1 53.6 %copy-start.12 = (f32[8,256]{1,0:T(8,128)S(1)}, f32[8,256]{1,0:T(8,128)}, u32[]{:S(2)}) copy-start(f32[8,256]{1,0:T(8,128)} %twiddle_ref.3) | copy-start | bytes 24580
  75.1 53.5 %all-to-all-start.1 = ((bf16[32,8,4096]{2,1,0:T(8,128)(2,1)}), bf16[32,8,4096]{2,1,0:T(8,128)(2,1)}, u32[]{:S(2)}, u32[]{:S(2)}) async-start(bf16[32,8,4096]{2,1,0:T(8,128)(2,1)} %bitcast.7), calls=%async_computation.1 | async-start | bytes 4194304 | tf_op jit(solution)/shard_map/all_to_all | solution.py:234
  135.5 4.1 %collective-permute-start = (bf16[512,384]{1,0:T(8,128)(2,1)S(1)}, bf16[512,384]{1,0:T(8,128)(2,1)S(1)}, u32[]{:S(2)}, u32[]{:S(2)}) collective-permute-start(bf16[512,384]{1,0:T(8,128)(2,1)S(1)} %broadcast_select_fusion), channel_id=1, source_target_pairs={{0,16},{16,0},{32,48},{48,32},{64,80},{80,64},{96,112},{112,96},{1... | collective-permute-start | bytes 1179656 | tf_op jit(solution)/shard_map/ppermute | solution.py:266
  201.8 7.8 %collective-permute-start.1 = (bf16[512,384]{1,0:T(8,128)(2,1)S(1)}, bf16[512,384]{1,0:T(8,128)(2,1)S(1)}, u32[]{:S(2)}, u32[]{:S(2)}) collective-permute-start(bf16[512,384]{1,0:T(8,128)(2,1)S(1)} %bitcast.16), channel_id=1, source_target_pairs={{0,16},{16,0},{32,48},{48,32},{64,80},{80,64},{96,112},{112,96},{1... | collective-permute-start | bytes 1179656 | tf_op jit(solution)/shard_map/ppermute | solution.py:276

commit v3 on v2

v3 whole, which is shorter than its diff:
```python
import functools

import jax
import jax.numpy as jnp
from jax import lax
from jax.experimental import pallas as pl
from jax.experimental.pallas import tpu as pltpu
from jax.sharding import PartitionSpec as P

F32 = jnp.float32
BF16 = jnp.bfloat16
LANES = 128
VMEM = pl.BlockSpec(memory_space=pltpu.VMEM)
HBM = pl.BlockSpec(memory_space=pl.ANY)


def params(mib):
    return pltpu.CompilerParams(vmem_limit_bytes=mib * 1024 * 1024)


def dot(a, b, dims=((1,), (0,))):
    return lax.dot_general(a, b, (dims, ((), ())), preferred_element_type=F32)


NT = ((1,), (1,))
TN = ((0,), (0,))


def every(ref, start, count, step):
    return ref[pl.ds(start, count, stride=step), :]


def place_major(ref, groups, places):
    return jnp.concatenate([every(ref, p, groups, places) for p in range(places)], axis=0)


def group_major(ref, value, groups, places):
    for p in range(places):
        ref[pl.ds(p, groups, stride=places), :] = value[p * groups : (p + 1) * groups]
    return ref[...]


def shuffle(outer, inner):
    size = outer * inner
    row = lax.broadcasted_iota(jnp.int32, (size, size), 0)
    column = lax.broadcasted_iota(jnp.int32, (size, size), 1)
    return jnp.where(column == (row % inner) * outer + row // inner, 1.0, 0.0).astype(BF16)


def rows_before(
    groups, x_hbm, ct_hbm, wv_hbm, wg_hbm, wo_hbm, right_hbm, twiddle_hbm,
    send_hbm,
    x_ref, ct_ref, wv_ref, wg_ref, wo_ref, right_ref, twiddle_ref,
    send_ref, wide, cols, small_sems, in_sems, send_sems,
):
    blocks = twiddle_ref.shape[0]
    size = right_ref.shape[0]
    places = size // groups
    width = x_ref.shape[1]
    parts = in_sems.shape[1]
    step = x_ref.shape[0] // parts
    small = [
        pltpu.make_async_copy(source, target, small_sems.at[n])
        for n, (source, target) in enumerate(
            (
                (wg_hbm, wg_ref), (wo_hbm, wo_ref), (wv_hbm, wv_ref),
                (right_hbm, right_ref), (twiddle_hbm, twiddle_ref),
            )
        )
    ]
    for copy in small:
        copy.start()
    copies = []
    for n in range(parts):
        rows = pl.ds(n * step, step)
        copies.append(
            (
                pltpu.make_async_copy(x_hbm.at[rows], x_ref.at[rows], in_sems.at[0, n]),
                pltpu.make_async_copy(ct_hbm.at[rows], ct_ref.at[rows], in_sems.at[1, n]),
            )
        )
        for copy in copies[-1]:
            copy.start()
    to_places = shuffle(places, groups)
    for copy in small:
        copy.wait()
    right = dot(to_places, right_ref[...]).astype(BF16)
    wide[...] = jnp.concatenate(
        [twiddle_ref[...], jnp.zeros((LANES - blocks, size), F32)], axis=0
    ).T
    twist = place_major(wide, groups, places)
    out = []
    for i in range(blocks):
        rows = slice(i * size, (i + 1) * size)
        if i * size % step == 0:
            for copy in copies[i * size // step]:
                copy.wait()
        x = x_ref[rows, :]
        gates = dot(x, wg_ref[...]).astype(BF16)
        back = dot(ct_ref[rows, :], wo_ref[...], NT).astype(BF16)
        values = dot(x, wv_ref[...]).astype(BF16)
        mixed = (back.astype(F32) * gates.astype(F32)).astype(BF16)
        mixed = dot(to_places, mixed).astype(BF16)
        twisted = (dot(right, values) * twist[:, i : i + 1]).astype(BF16)
        for p in range(places):
            part = slice(p * groups, (p + 1) * groups)
            here = slice(i * groups, (i + 1) * groups)
            cols[here, p * width : (p + 1) * width] = mixed[part]
            cols[here, (places + p) * width : (places + p + 1) * width] = twisted[part]
    to_send = shuffle(groups, blocks)
    lanes = cols.shape[1] // send_sems.shape[0]
    for n in range(send_sems.shape[0]):
        at = slice(n * lanes, (n + 1) * lanes)
        send_ref[:, at] = dot(to_send, cols[:, at]).astype(BF16)
        part = pl.ds(n * lanes, lanes)
        out.append(
            pltpu.make_async_copy(send_ref.at[:, part], send_hbm.at[:, part], send_sems.at[n])
        )
        out[-1].start()
    for copy in out:
        copy.wait()


def columns(left_ref, cols_ref, send_ref, grad_ref):
    left = left_ref[...]
    half = cols_ref.shape[1] // 2
    for at in range(0, half, 512):
        back = cols_ref[:, at : at + 512]
        twist = cols_ref[:, half + at : half + at + 512]
        send_ref[:, at : at + 512] = dot(left, back, TN).astype(BF16)
        send_ref[:, half + at : half + at + 512] = dot(left, twist).astype(BF16)
    grad_ref[...] = dot(cols_ref[:, :half], cols_ref[:, half:], NT)


def rows_after(
    groups, came_hbm, x_hbm, ct_hbm, wv_hbm, wg_hbm, wo_hbm, right_hbm, twiddle_hbm, left_grad_hbm,
    gi_hbm, keep_hbm, give_hbm,
    gi_ref, low_ref, high_ref, came_ref, x_ref, ct_ref,
    wv_ref, wg_ref, wo_ref, right_ref, twiddle_ref, left_grad_ref,
    wide, cols, gated_all, back_gates_all, back_values_all,
    came_sems, small_sems, in_sems, out_sems, half_sems,
):
    size = right_ref.shape[0]
    blocks = twiddle_ref.shape[0]
    places = size // groups
    width = x_ref.shape[1]
    small = [
        pltpu.make_async_copy(source, target, small_sems.at[n])
        for n, (source, target) in enumerate(
            (
                (right_hbm, right_ref), (twiddle_hbm, twiddle_ref), (wv_hbm, wv_ref),
                (wg_hbm, wg_ref), (wo_hbm, wo_ref), (left_grad_hbm, left_grad_ref),
            )
        )
    ]
    for copy in small[:2]:
        copy.start()
    parts = came_sems.shape[0]
    lanes = came_ref.shape[1] // parts
    came = []
    for n in range(parts):
        at = pl.ds(n * lanes, lanes)
        came.append(
            pltpu.make_async_copy(came_hbm.at[:, at], came_ref.at[:, at], came_sems.at[n])
        )
        came[-1].start()
    for copy in small[2:]:
        copy.start()
    pieces = in_sems.shape[1]
    step = x_ref.shape[0] // pieces
    local = []
    for n in range(pieces):
        at = pl.ds(n * step, step)
        local.append(
            (
                pltpu.make_async_copy(x_hbm.at[at], x_ref.at[at], in_sems.at[0, n]),
                pltpu.make_async_copy(ct_hbm.at[at], ct_ref.at[at], in_sems.at[1, n]),
            )
        )
        for copy in local[-1]:
            copy.start()
    to_blocks = shuffle(blocks, groups)
    to_groups = shuffle(groups, places)
    for copy in small[:2]:
        copy.wait()
    right = dot(shuffle(places, groups), right_ref[...]).astype(BF16)
    right_turned = right.T
    wide[...] = jnp.concatenate(
        [twiddle_ref[...], jnp.zeros((LANES - blocks, size), F32)], axis=0
    ).T
    twist = place_major(wide, groups, places)
    for n in range(parts):
        at = slice(n * lanes, (n + 1) * lanes)
        came[n].wait()
        cols[:, at] = dot(to_blocks, came_ref[:, at]).astype(BF16)
    for copy in small[2:]:
        copy.wait()
    lane = lax.broadcasted_iota(jnp.int32, (size, LANES), 1)
    twist_grad = jnp.zeros((size, LANES), F32)
    right_grad = jnp.zeros((size, size), F32)
    out = []
    for i in range(blocks):
        rows = slice(i * size, (i + 1) * size)
        here = slice(i * groups, (i + 1) * groups)
        n = i * size // step
        if i * size % step == 0:
            for copy in local[n]:
                copy.wait()
        x = x_ref[rows, :]
        values = dot(x, wv_ref[...]).astype(BF16)
        gates = dot(x, wg_ref[...]).astype(BF16)
        back_gated = dot(ct_ref[rows, :], wo_ref[...], NT).astype(BF16)
        back, mixed = (
            jnp.concatenate(
                [
                    cols[here, (first + p) * width : (first + p + 1) * width]
                    for p in range(places)
                ],
                axis=0,
            )
            for first in (0, places)
        )
        back = back.astype(F32)
        column = jnp.sum(back * dot(right, values), axis=1, keepdims=True)
        twist_grad = jnp.where(lane == i, column, twist_grad)
        back_rotated = (back * twist[:, i : i + 1]).astype(BF16)
        back_values = dot(right_turned, back_rotated).astype(BF16)
        right_grad += dot(back_rotated, values, NT)
        mixed = dot(to_groups, mixed)
        back_gates = (back_gated.astype(F32) * mixed).astype(BF16)
        gated_all[rows, :] = (gates.astype(F32) * mixed).astype(BF16)
        back_gates_all[rows, :] = back_gates
        back_values_all[rows, :] = back_values
        gi_ref[rows, :] = (
            dot(back_values, wv_ref[...], NT) + dot(back_gates, wg_ref[...], NT)
        ).astype(BF16)
        if (i + 1) * size % step == 0:
            at = pl.ds(n * step, step)
            out.append(pltpu.make_async_copy(gi_ref.at[at], gi_hbm.at[at], out_sems.at[n]))
            out[-1].start()

    def put(ref, tile, grad):
        for h in range(2):
            ref[h * size : (h + 1) * size, tile * LANES : (tile + 1) * LANES] = grad[
                :, h * LANES : (h + 1) * LANES
            ].astype(BF16)

    put(low_ref, 0, dot(x_ref[...], back_values_all[...], TN))
    put(high_ref, 0, dot(x_ref[...], back_gates_all[...], TN))
    put(low_ref, 1, dot(gated_all[...], ct_ref[...], TN))
    put(high_ref, 2, left_grad_ref[...])
    for h in range(2):
        half = group_major(wide, right_grad[:, h * LANES : (h + 1) * LANES], groups, places)
        low_ref[h * size : (h + 1) * size, 2 * LANES :] = half.astype(BF16)
    flat = group_major(wide, twist_grad, groups, places).T[:blocks]
    own = jnp.concatenate([flat[:, :LANES], flat[:, LANES:]], axis=0).astype(BF16)
    high_ref[:, LANES : 2 * LANES] = jnp.zeros((2 * size, LANES), BF16)
    at = pl.multiple_of(lax.axis_index("seq") * 2 * blocks, 2 * blocks)
    high_ref[pl.ds(at, 2 * blocks), LANES : 2 * LANES] = own

    def leave(keep, give):
        copies = (
            pltpu.make_async_copy(keep, keep_hbm, half_sems.at[0]),
            pltpu.make_async_copy(give, give_hbm, half_sems.at[1]),
        )
        for copy in copies:
            copy.start()
        for copy in copies:
            copy.wait()

    even = lax.axis_index("seq") % 2 == 0

    @pl.when(even)
    def _():
        leave(low_ref, high_ref)

    @pl.when(jnp.logical_not(even))
    def _():
        leave(high_ref, low_ref)

    for copy in out:
        copy.wait()


def unpack(mine_ref, other_ref, value_ref, gate_ref, out_ref, right_ref, left_ref, twiddle_ref):
    size = value_ref.shape[0]
    blocks = twiddle_ref.shape[0]
    seq = lax.axis_index("seq")

    def take(ref, source, tile):
        for h in range(2):
            ref[:, h * LANES : (h + 1) * LANES] = source[
                h * size : (h + 1) * size, tile * LANES : (tile + 1) * LANES
            ].astype(F32)

    def spread(low, high):
        take(value_ref, low, 0)
        take(out_ref, low, 1)
        take(right_ref, low, 2)
        take(gate_ref, high, 0)
        take(left_ref, high, 2)
        at = pl.multiple_of(seq * 2 * blocks, 2 * blocks)
        own = high[pl.ds(at, 2 * blocks), LANES : 2 * LANES].astype(F32)
        twiddle_ref[:, :LANES] = own[:blocks]
        twiddle_ref[:, LANES:] = own[blocks:]

    @pl.when(seq % 2 == 0)
    def _():
        spread(mine_ref, other_ref)

    @pl.when(seq % 2 == 1)
    def _():
        spread(other_ref, mine_ref)


def shape(*dims, dtype=BF16):
    return jax.ShapeDtypeStruct(dims, dtype)


def cost(flops, moved):
    return pl.CostEstimate(flops=int(flops), bytes_accessed=int(moved), transcendentals=0)


def on_device(sizes, inputs, w_value, w_gate, w_out, mon_right, mon_left, twiddle, cotangent):
    seq_size, chan_size, dp_size = sizes
    _, length, width = inputs.shape
    size = mon_right.shape[0]
    blocks = length // size
    places = size // seq_size
    x, ct = inputs[0], cotangent[0]
    cols = places * width
    square = 2 * length * width * width

    cube = shape(length, width)
    weights = [pltpu.VMEM((width, width), BF16)] * 3
    tables = weights + [pltpu.VMEM((size, size), BF16), pltpu.VMEM((blocks, size), F32)]
    activations = pltpu.VMEM((length, width), BF16)
    exchanged = pltpu.VMEM((seq_size * blocks, 2 * cols), BF16)
    small = (w_value[0], w_gate[0], w_out[0], mon_right, twiddle)
    send = pl.pallas_call(
        functools.partial(rows_before, seq_size),
        out_shape=shape(seq_size * blocks, 2 * cols),
        in_specs=[HBM] * 7,
        out_specs=HBM,
        scratch_shapes=[
            activations, activations, *tables, exchanged,
            pltpu.VMEM((size, LANES), F32),
            exchanged,
            pltpu.SemaphoreType.DMA((5,)),
            pltpu.SemaphoreType.DMA((2, 4)),
            pltpu.SemaphoreType.DMA((8,)),
        ],
        compiler_params=params(60),
        cost_estimate=cost(4 * square, 8 * length * width),
        name="rows_before",
    )(x, ct, *small)
    came = lax.all_to_all(send, "seq", 0, 0, tiled=True)
    send_back, left_part = pl.pallas_call(
        columns,
        out_shape=(shape(seq_size * blocks, 2 * cols), shape(size, size, dtype=F32)),
        in_specs=[VMEM] * 2,
        out_specs=(VMEM,) * 2,
        compiler_params=params(20),
        cost_estimate=cost(3 * square, 8 * length * width),
        name="columns",
    )(mon_left, came)
    came_back = lax.all_to_all(send_back, "seq", 0, 0, tiled=True)
    half = shape(2 * size, 3 * LANES)
    grad_inputs, keep, give = pl.pallas_call(
        functools.partial(rows_after, seq_size),
        out_shape=(shape(length, width), half, half),
        in_specs=[HBM] * 9,
        out_specs=(HBM,) * 3,
        scratch_shapes=[
            activations,
            pltpu.VMEM(half.shape, BF16),
            pltpu.VMEM(half.shape, BF16),
            exchanged, activations, activations, *tables,
            pltpu.VMEM((size, size), F32),
            pltpu.VMEM((size, LANES), F32),
            exchanged, activations, activations, activations,
            pltpu.SemaphoreType.DMA((8,)),
            pltpu.SemaphoreType.DMA((6,)),
            pltpu.SemaphoreType.DMA((2, 4)),
            pltpu.SemaphoreType.DMA((4,)),
            pltpu.SemaphoreType.DMA((2,)),
        ],
        compiler_params=params(60),
        cost_estimate=cost(11 * square, 12 * length * width),
        name="rows_after",
    )(came_back, x, ct, *small, left_part)

    even = lax.axis_index("seq") % 2 == 0
    swap = [(i, i ^ 1) for i in range(seq_size)]
    like = [
        [seq * dp_size + dp for seq in range(core, seq_size, 2) for dp in range(dp_size)]
        for core in range(2)
    ]
    peers = len(like[0])
    theirs = lax.ppermute(give, "seq", swap)
    pair = (keep.astype(F32) + theirs.astype(F32)).astype(BF16)
    arrived = lax.all_to_all(pair, ("seq", "dp"), 0, 0, tiled=True, axis_index_groups=like)
    mine = jnp.sum(arrived.reshape(peers, -1, 3 * LANES).astype(F32), axis=0)
    factors = mine[None, :, LANES:].astype(BF16)
    factors = jnp.broadcast_to(factors, (chan_size,) + factors.shape[1:])
    factors = lax.all_to_all(factors, "chan", 0, 0, tiled=True).astype(F32)
    factors = jnp.sum(factors, axis=0)
    middle = jnp.where(even, mine[:, LANES : 2 * LANES], factors[:, :LANES])
    done = jnp.concatenate([mine[:, :LANES], middle, factors[:, LANES:]], axis=1).astype(BF16)
    spread = jnp.broadcast_to(done[None], (peers,) + done.shape).reshape(pair.shape)
    half = lax.all_to_all(spread, ("seq", "dp"), 0, 0, tiled=True, axis_index_groups=like)
    other = lax.ppermute(half, "seq", swap)
    g_value, g_gate, g_out, g_right, g_left, g_twiddle = pl.pallas_call(
        unpack,
        out_shape=(shape(size, size, dtype=F32),) * 5 + (shape(blocks, size, dtype=F32),),
        in_specs=[VMEM] * 2,
        out_specs=(VMEM,) * 6,
        compiler_params=params(20),
        name="unpack",
    )(half, other)
    return grad_inputs[None], g_value[None], g_gate[None], g_out[None], g_right, g_left, g_twiddle


def solution(mesh):
    sizes = tuple(mesh.shape[name] for name in ("seq", "chan", "dp"))
    return jax.shard_map(
        functools.partial(on_device, sizes),
        mesh=mesh,
        in_specs=(
            P("dp", "seq", "chan"),
            P("chan", None, None),
            P("chan", None, None),
            P("chan", None, None),
            P(),
            P(),
            P("seq", None),
            P("dp", "seq", "chan"),
        ),
        out_specs=(
            P("dp", "seq", "chan"),
            P("chan", None, None),
            P("chan", None, None),
            P("chan", None, None),
            P(),
            P(),
            P("seq", None),
        ),
        check_vma=False,
    )
```

time: 211 us -> 209 us (level)
  waiting for transfers between devices: 50.8 us -> 14.7 us
  blocking collectives: 122 us -> 152 us
  starting transfers between devices: 14.6 us -> 20.5 us
  local copies, waits for them, and re-layouts: 4.4 us -> 0.66 us
    all_to_all x1, waiting for transfers between devices: 48.2 us -> 11.5 us  [on_device(): factors = lax.all_to_all(factors, 'chan', 0, 0, tiled=True).astype(F32)]
    all_to_all x1, blocking collectives: 23.8 us -> 54.1 us  [on_device(): came_back = lax.all_to_all(send_back, 'seq', 0, 0, tiled=True)]
    all_to_all x1, starting transfers between devices: 5.32 us -> 12.1 us  [on_device(): factors = lax.all_to_all(factors, 'chan', 0, 0, tiled=True).astype(F32)]
    unnamed x30 -> x4, local copies, waits for them, and re-layouts: 4.35 us -> 0.01 us
    pallas_call x1, Pallas kernels: 3.96 us -> 1 us  [on_device(): pl.pallas_call(columns, out_shape=(shape(seq_size * blocks, 2 * cols), sh...]
    pallas_call x1, Pallas kernels: 6.83 us -> 9.53 us  [on_device(): pl.pallas_call(functools.partial(rows_after, seq_size), out_shape=(shape(...]
where the time goes in v3:
time: 209 us; the launch traced here: 208 us
  blocking collectives  152 us (73%)
  starting transfers between devices  20.5 us (10%)
  Pallas kernels  18.2 us (9%)
  waiting for transfers between devices  14.7 us (7%)
    all_to_all x1, blocking collectives, on_device(): came = lax.all_to_all(send, 'seq', 0, 0, tiled=True)  59.8 us
    all_to_all x1, blocking collectives, on_device(): came_back = lax.all_to_all(send_back, 'seq', 0, 0, tiled=True)  54.1 us
    all_to_all x1, blocking collectives, on_device(): lax.all_to_all(pair, ('seq', 'dp'), 0, 0, tiled=True, axis_index_groups=l...  20.8 us
    all_to_all x1, blocking collectives, on_device(): lax.all_to_all(spread, ('seq', 'dp'), 0, 0, tiled=True, axis_index_groups...  17.5 us
    all_to_all x1, starting transfers between devices, on_device(): factors = lax.all_to_all(factors, 'chan', 0, 0, tiled=True).astype(F32)  12.1 us
    all_to_all x1, waiting for transfers between devices, on_device(): factors = lax.all_to_all(factors, 'chan', 0, 0, tiled=True).astype(F32)  11.5 us
    pallas_call x1, Pallas kernels, on_device(): pl.pallas_call(functools.partial(rows_after, seq_size), out_shape=(shape(...  9.53 us
    pallas_call x1, Pallas kernels, on_device(): pl.pallas_call(functools.partial(rows_before, seq_size), out_shape=shape(...  6.5 us
  transfers between devices with their start and end apart: 3, of which 3 were waited for; matrix products, arithmetic and copies ran while one was open for 0% of the time, Pallas kernels for 0%

profile of v3, /device:TPU:1, one launch (start us, length us, event | category | flops | bytes accessed | tf_op | source)
XLA Modules:
  0.0 208.3 jit_solution(15983830019393827136)
XLA Ops:
  0.6 6.5 %rows_before.1 = bf16[256,4096]{1,0:T(8,128)(2,1)} custom-call(bf16[2048,256]{1,0:T(8,128)(2,1)} %bitcast.22, bf16[2048,256]{1,0:T(8,128)(2,1)} %bitcast.24, bf16[256,256]{1,0:T(8,128)(2,1)} %bitcast.26, bf16[256,256]{1,0:T(8,128)(2,1)} %bitcast.28, bf16[256,256]{1,0:T(8,128)(2,1)} %bitcast.30, bf16[256,256]{1,0:T(8,128)(2,1)} %right_hbm.3, f32[8,256]{1,0:T(8,128)} %twiddle_hbm.3), custom_call_target="tpu_custom_call" | custom-call | flops 1073741824 | bytes 4194304 | tf_op jit(solution)/shard_map/rows_before/pallas_call | solution.py:340
  7.1 0.0 copy-start
  7.2 59.8 %all_to_all.44 = bf16[32,8,4096]{2,1,0:T(8,128)(2,1)S(1)} all-to-all(bf16[32,8,4096]{2,1,0:T(8,128)(2,1)} %bitcast.20), channel_id=1, replica_groups=mesh['seq'=32,'chan'=4,'dp'=4] {'seq'}, dimensions={0} | all-to-all | bytes 4194304 | tf_op jit(solution)/shard_map/all_to_all | solution.py:357
  67.0 0.0 copy-done
  67.0 1.0 columns.1
  68.0 0.0 copy-start.1
  68.0 54.1 %all_to_all.45 = bf16[32,8,4096]{2,1,0:T(8,128)(2,1)} all-to-all(bf16[32,8,4096]{2,1,0:T(8,128)(2,1)S(1)} %bitcast.17), channel_id=1, replica_groups=mesh['seq'=32,'chan'=4,'dp'=4] {'seq'}, dimensions={0} | all-to-all | bytes 4194304 | tf_op jit(solution)/shard_map/all_to_all | solution.py:367
  122.1 0.0 copy-done.1
  122.1 9.5 %rows_after.1 = (bf16[2048,256]{1,0:T(8,128)(2,1)}, bf16[512,384]{1,0:T(8,128)(2,1)}, bf16[512,384]{1,0:T(8,128)(2,1)}) custom-call(bf16[256,4096]{1,0:T(8,128)(2,1)} %bitcast.21, bf16[2048,256]{1,0:T(8,128)(2,1)} %bitcast.23, bf16[2048,256]{1,0:T(8,128)(2,1)} %bitcast.25, bf16[256,256]{1,0:T(8,128)(2,1)} %bitcast.27, bf16[256,256]{1,0:T(8,128)(2,1)} %bitcast.29, ...), custom_call_target="tpu_custom_call" | custom-call | flops 2952790016 | bytes 6291456 | tf_op jit(solution)/shard_map/rows_after/pallas_call | solution.py:369
  131.6 1.9 collective-permute-start
  133.6 1.9 collective-permute-done
  135.5 1.1 fusion
  136.6 20.8 %all_to_all.46 = bf16[64,8,384]{2,1,0:T(8,128)(2,1)S(1)} all-to-all(bf16[64,8,384]{2,1,0:T(8,128)(2,1)S(1)} %fusion), channel_id=1, replica_groups={{0,1,2,3,32,33,34,35,64,65,66,67,96,97,98,99,128,129,130,131,160,161,16..., dimensions={0} | all-to-all | bytes 786432 | tf_op jit(solution)/shard_map/all_to_all | solution.py:402
  157.4 0.1 convert_reduce_fusion
  157.5 0.6 broadcast_in_dim.25
  158.1 12.1 %all-to-all-start.3 = ((bf16[4,8,256]{2,1,0:T(8,128)(2,1)}), bf16[4,8,256]{2,1,0:T(8,128)(2,1)S(1)}, u32[]{:S(2)}, u32[]{:S(2)}) async-start(bf16[4,8,256]{2,1,0:T(8,128)(2,1)} %broadcast_in_dim.25), calls=%async_computation.3 | async-start | bytes 32768 | tf_op jit(solution)/shard_map/all_to_all | solution.py:406
  170.2 11.5 %all-to-all-done.3 = bf16[4,8,256]{2,1,0:T(8,128)(2,1)S(1)} async-done(((bf16[4,8,256]{2,1,0:T(8,128)(2,1)}), bf16[4,8,256]{2,1,0:T(8,128)(2,1)S(1)}, u32[]{:S(2)}, u32[]{:S(2)}) %all-to-all-start.3) | async-done | bytes 16416 | tf_op jit(solution)/shard_map/all_to_all | solution.py:406
  181.8 17.5 %all_to_all.47 = bf16[64,8,384]{2,1,0:T(8,128)(2,1)S(1)} all-to-all(bf16[64,8,384]{2,1,0:T(8,128)(2,1)S(1)} %broadcast_in_dim.26), channel_id=1, replica_groups={{0,1,2,3,32,33,34,35,64,65,66,67,96,97,98,99,128,129,130,131,160,161,16..., dimensions={0} | all-to-all | bytes 786432 | tf_op jit(solution)/shard_map/all_to_all | solution.py:411
  199.3 6.5 %collective-permute-start.1 = (bf16[512,384]{1,0:T(8,128)(2,1)S(1)}, bf16[512,384]{1,0:T(8,128)(2,1)S(1)}, u32[]{:S(2)}, u32[]{:S(2)}) collective-permute-start(bf16[512,384]{1,0:T(8,128)(2,1)S(1)} %bitcast.18), channel_id=1, source_target_pairs={{0,16},{16,0},{32,48},{48,32},{64,80},{80,64},{96,112},{112,96},{1... | collective-permute-start | bytes 1179656 | tf_op jit(solution)/shard_map/ppermute | solution.py:412
  205.8 1.3 collective-permute-done.1.other_ref
  207.1 1.1 unpack.1
  (5 shorter events, 0.1 us)
Async XLA Ops:
  7.1 59.9 %copy-start = (bf16[256,256]{1,0:T(8,128)(2,1)S(1)}, bf16[256,256]{1,0:T(8,128)(2,1)}, u32[]{:S(2)}) copy-start(bf16[256,256]{1,0:T(8,128)(2,1)} %left_ref.1) | copy-start | bytes 393220
  68.0 54.1 %copy-start.1 = (f32[256,256]{1,0:T(8,128)}, f32[256,256]{1,0:T(8,128)S(1)}, u32[]{:S(2)}) copy-start(f32[256,256]{1,0:T(8,128)S(1)} %get-tuple-element.19.left_grad_hbm) | copy-start | bytes 786436
  131.6 3.8 %collective-permute-start = (bf16[512,384]{1,0:T(8,128)(2,1)}, bf16[512,384]{1,0:T(8,128)(2,1)S(1)}, u32[]{:S(2)}, u32[]{:S(2)}) collective-permute-start(bf16[512,384]{1,0:T(8,128)(2,1)} %get-tuple-element.22), channel_id=1, source_target_pairs={{0,16},{16,0},{32,48},{48,32},{64,80},{80,64},{96,112},{112,96},{1... | collective-permute-start | bytes 1179656 | tf_op jit(solution)/shard_map/ppermute | solution.py:400
  158.1 23.6 %all-to-all-start.3 = ((bf16[4,8,256]{2,1,0:T(8,128)(2,1)}), bf16[4,8,256]{2,1,0:T(8,128)(2,1)S(1)}, u32[]{:S(2)}, u32[]{:S(2)}) async-start(bf16[4,8,256]{2,1,0:T(8,128)(2,1)} %broadcast_in_dim.25), calls=%async_computation.3 | async-start | bytes 32768 | tf_op jit(solution)/shard_map/all_to_all | solution.py:406
  199.3 7.8 %collective-permute-start.1 = (bf16[512,384]{1,0:T(8,128)(2,1)S(1)}, bf16[512,384]{1,0:T(8,128)(2,1)S(1)}, u32[]{:S(2)}, u32[]{:S(2)}) collective-permute-start(bf16[512,384]{1,0:T(8,128)(2,1)S(1)} %bitcast.18), channel_id=1, source_target_pairs={{0,16},{16,0},{32,48},{48,32},{64,80},{80,64},{96,112},{112,96},{1... | collective-permute-start | bytes 1179656 | tf_op jit(solution)/shard_map/ppermute | solution.py:412

commit v4 on v3

--- a/solution.py
+++ b/solution.py
@@ -49,9 +49,9 @@
 
 def rows_before(
     groups, x_hbm, ct_hbm, wv_hbm, wg_hbm, wo_hbm, right_hbm, twiddle_hbm,
-    send_hbm,
+    send_hbm, value_hbm, gate_hbm, back_hbm,
     x_ref, ct_ref, wv_ref, wg_ref, wo_ref, right_ref, twiddle_ref,
-    send_ref, wide, cols, small_sems, in_sems, send_sems,
+    send_ref, value_ref, gate_ref, back_ref, wide, cols, small_sems, in_sems, out_sems, send_sems,
 ):
     blocks = twiddle_ref.shape[0]
     size = right_ref.shape[0]
@@ -99,6 +99,19 @@
         gates = dot(x, wg_ref[...]).astype(BF16)
         back = dot(ct_ref[rows, :], wo_ref[...], NT).astype(BF16)
         values = dot(x, wv_ref[...]).astype(BF16)
+        gate_ref[rows, :] = gates
+        back_ref[rows, :] = back
+        value_ref[rows, :] = values
+        if (i + 1) * size % step == 0:
+            n = i * size // step
+            done = pl.ds(n * step, step)
+            for k, (source, target) in enumerate(
+                ((gate_ref, gate_hbm), (back_ref, back_hbm), (value_ref, value_hbm))
+            ):
+                out.append(
+                    pltpu.make_async_copy(source.at[done], target.at[done], out_sems.at[k, n])
+                )
+                out[-1].start()
         mixed = (back.astype(F32) * gates.astype(F32)).astype(BF16)
         mixed = dot(to_places, mixed).astype(BF16)
         twisted = (dot(right, values) * twist[:, i : i + 1]).astype(BF16)
@@ -132,84 +145,42 @@
     grad_ref[...] = dot(cols_ref[:, :half], cols_ref[:, half:], NT)
 
 
+def input_grad(back_value_ref, back_gate_ref, wv_ref, wg_ref, gi_ref):
+    for at in range(0, gi_ref.shape[0], 256):
+        rows = slice(at, at + 256)
+        gi_ref[rows, :] = (
+            dot(back_value_ref[rows, :], wv_ref[...], NT)
+            + dot(back_gate_ref[rows, :], wg_ref[...], NT)
+        ).astype(BF16)
+
+
 def rows_after(
-    groups, came_hbm, x_hbm, ct_hbm, wv_hbm, wg_hbm, wo_hbm, right_hbm, twiddle_hbm, left_grad_hbm,
-    gi_hbm, keep_hbm, give_hbm,
-    gi_ref, low_ref, high_ref, came_ref, x_ref, ct_ref,
-    wv_ref, wg_ref, wo_ref, right_ref, twiddle_ref, left_grad_ref,
-    wide, cols, gated_all, back_gates_all, back_values_all,
-    came_sems, small_sems, in_sems, out_sems, half_sems,
+    groups, came_ref, x_ref, ct_ref, value_ref, gate_ref, back_ref, right_ref, twiddle_ref,
+    left_grad_ref,
+    back_value_ref, back_gate_ref, keep_ref, give_ref,
+    low_ref, high_ref, wide, cols, gated_all, rotated_all, turned_all,
 ):
     size = right_ref.shape[0]
     blocks = twiddle_ref.shape[0]
     places = size // groups
     width = x_ref.shape[1]
-    small = [
-        pltpu.make_async_copy(source, target, small_sems.at[n])
-        for n, (source, target) in enumerate(
-            (
-                (right_hbm, right_ref), (twiddle_hbm, twiddle_ref), (wv_hbm, wv_ref),
-                (wg_hbm, wg_ref), (wo_hbm, wo_ref), (left_grad_hbm, left_grad_ref),
-            )
-        )
-    ]
-    for copy in small[:2]:
-        copy.start()
-    parts = came_sems.shape[0]
-    lanes = came_ref.shape[1] // parts
-    came = []
-    for n in range(parts):
-        at = pl.ds(n * lanes, lanes)
-        came.append(
-            pltpu.make_async_copy(came_hbm.at[:, at], came_ref.at[:, at], came_sems.at[n])
-        )
-        came[-1].start()
-    for copy in small[2:]:
-        copy.start()
-    pieces = in_sems.shape[1]
-    step = x_ref.shape[0] // pieces
-    local = []
-    for n in range(pieces):
-        at = pl.ds(n * step, step)
-        local.append(
-            (
-                pltpu.make_async_copy(x_hbm.at[at], x_ref.at[at], in_sems.at[0, n]),
-                pltpu.make_async_copy(ct_hbm.at[at], ct_ref.at[at], in_sems.at[1, n]),
-            )
-        )
-        for copy in local[-1]:
-            copy.start()
     to_blocks = shuffle(blocks, groups)
     to_groups = shuffle(groups, places)
-    for copy in small[:2]:
-        copy.wait()
     right = dot(shuffle(places, groups), right_ref[...]).astype(BF16)
     right_turned = right.T
     wide[...] = jnp.concatenate(
         [twiddle_ref[...], jnp.zeros((LANES - blocks, size), F32)], axis=0
     ).T
     twist = place_major(wide, groups, places)
-    for n in range(parts):
-        at = slice(n * lanes, (n + 1) * lanes)
-        came[n].wait()
-        cols[:, at] = dot(to_blocks, came_ref[:, at]).astype(BF16)
-    for copy in small[2:]:
-        copy.wait()
+    for at in range(0, cols.shape[1], 512):
+        cols[:, at : at + 512] = dot(to_blocks, came_ref[:, at : at + 512]).astype(BF16)
     lane = lax.broadcasted_iota(jnp.int32, (size, LANES), 1)
     twist_grad = jnp.zeros((size, LANES), F32)
-    right_grad = jnp.zeros((size, size), F32)
-    out = []
     for i in range(blocks):
         rows = slice(i * size, (i + 1) * size)
         here = slice(i * groups, (i + 1) * groups)
-        n = i * size // step
-        if i * size % step == 0:
-            for copy in local[n]:
-                copy.wait()
-        x = x_ref[rows, :]
-        values = dot(x, wv_ref[...]).astype(BF16)
-        gates = dot(x, wg_ref[...]).astype(BF16)
-        back_gated = dot(ct_ref[rows, :], wo_ref[...], NT).astype(BF16)
+        values = value_ref[rows, :]
+        turned_all[rows, :] = values.T
         back, mixed = (
             jnp.concatenate(
                 [
@@ -224,20 +195,11 @@
         column = jnp.sum(back * dot(right, values), axis=1, keepdims=True)
         twist_grad = jnp.where(lane == i, column, twist_grad)
         back_rotated = (back * twist[:, i : i + 1]).astype(BF16)
-        back_values = dot(right_turned, back_rotated).astype(BF16)
-        right_grad += dot(back_rotated, values, NT)
+        rotated_all[:, rows] = back_rotated
+        back_value_ref[rows, :] = dot(right_turned, back_rotated).astype(BF16)
         mixed = dot(to_groups, mixed)
-        back_gates = (back_gated.astype(F32) * mixed).astype(BF16)
-        gated_all[rows, :] = (gates.astype(F32) * mixed).astype(BF16)
-        back_gates_all[rows, :] = back_gates
-        back_values_all[rows, :] = back_values
-        gi_ref[rows, :] = (
-            dot(back_values, wv_ref[...], NT) + dot(back_gates, wg_ref[...], NT)
-        ).astype(BF16)
-        if (i + 1) * size % step == 0:
-            at = pl.ds(n * step, step)
-            out.append(pltpu.make_async_copy(gi_ref.at[at], gi_hbm.at[at], out_sems.at[n]))
-            out[-1].start()
+        back_gate_ref[rows, :] = (back_ref[rows, :].astype(F32) * mixed).astype(BF16)
+        gated_all[rows, :] = (gate_ref[rows, :].astype(F32) * mixed).astype(BF16)
 
     def put(ref, tile, grad):
         for h in range(2):
@@ -245,10 +207,11 @@
                 :, h * LANES : (h + 1) * LANES
             ].astype(BF16)
 
-    put(low_ref, 0, dot(x_ref[...], back_values_all[...], TN))
-    put(high_ref, 0, dot(x_ref[...], back_gates_all[...], TN))
+    put(low_ref, 0, dot(x_ref[...], back_value_ref[...], TN))
+    put(high_ref, 0, dot(x_ref[...], back_gate_ref[...], TN))
     put(low_ref, 1, dot(gated_all[...], ct_ref[...], TN))
     put(high_ref, 2, left_grad_ref[...])
+    right_grad = dot(rotated_all[...], turned_all[...])
     for h in range(2):
         half = group_major(wide, right_grad[:, h * LANES : (h + 1) * LANES], groups, places)
         low_ref[h * size : (h + 1) * size, 2 * LANES :] = half.astype(BF16)
@@ -258,28 +221,36 @@
     at = pl.multiple_of(lax.axis_index("seq") * 2 * blocks, 2 * blocks)
     high_ref[pl.ds(at, 2 * blocks), LANES : 2 * LANES] = own
 
-    def leave(keep, give):
-        copies = (
-            pltpu.make_async_copy(keep, keep_hbm, half_sems.at[0]),
-            pltpu.make_async_copy(give, give_hbm, half_sems.at[1]),
-        )
-        for copy in copies:
-            copy.start()
-        for copy in copies:
-            copy.wait()
-
     even = lax.axis_index("seq") % 2 == 0
 
     @pl.when(even)
     def _():
-        leave(low_ref, high_ref)
+        keep_ref[...] = low_ref[...]
+        give_ref[...] = high_ref[...]
 
     @pl.when(jnp.logical_not(even))
     def _():
-        leave(high_ref, low_ref)
-
-    for copy in out:
-        copy.wait()
+        keep_ref[...] = high_ref[...]
+        give_ref[...] = low_ref[...]
+
+
+def sum_peers(came_ref, mine_ref, factors_ref):
+    rows, lanes = mine_ref.shape
+    total = jnp.sum(came_ref[...].astype(F32).reshape(-1, rows, lanes), axis=0)
+    mine_ref[...] = total
+    copies = factors_ref.shape[0] // rows
+    factors_ref[...] = jnp.concatenate([total[:, LANES:]] * copies, axis=0).astype(BF16)
+
+
+def sum_factors(mine_ref, came_ref, done_ref):
+    rows, lanes = mine_ref.shape
+    total = jnp.sum(came_ref[...].astype(F32).reshape(-1, rows, lanes - LANES), axis=0)
+    even = lax.axis_index("seq") % 2 == 0
+    middle = jnp.where(even, mine_ref[:, LANES : 2 * LANES], total[:, :LANES])
+    done = jnp.concatenate([mine_ref[:, :LANES], middle, total[:, LANES:]], axis=1)
+    pair = jnp.concatenate([done, done], axis=0).astype(BF16)
+    for at in range(0, done_ref.shape[0], 2 * rows):
+        done_ref[at : at + 2 * rows, :] = pair
 
 
 def unpack(mine_ref, other_ref, value_ref, gate_ref, out_ref, right_ref, left_ref, twiddle_ref):
@@ -337,21 +308,23 @@
     activations = pltpu.VMEM((length, width), BF16)
     exchanged = pltpu.VMEM((seq_size * blocks, 2 * cols), BF16)
     small = (w_value[0], w_gate[0], w_out[0], mon_right, twiddle)
-    send = pl.pallas_call(
+    cube = shape(length, width)
+    send, values, gates, back_gated = pl.pallas_call(
         functools.partial(rows_before, seq_size),
-        out_shape=shape(seq_size * blocks, 2 * cols),
+        out_shape=(shape(seq_size * blocks, 2 * cols), cube, cube, cube),
         in_specs=[HBM] * 7,
-        out_specs=HBM,
+        out_specs=(HBM,) * 4,
         scratch_shapes=[
-            activations, activations, *tables, exchanged,
+            activations, activations, *tables, exchanged, activations, activations, activations,
             pltpu.VMEM((size, LANES), F32),
             exchanged,
             pltpu.SemaphoreType.DMA((5,)),
             pltpu.SemaphoreType.DMA((2, 4)),
+            pltpu.SemaphoreType.DMA((3, 4)),
             pltpu.SemaphoreType.DMA((8,)),
         ],
         compiler_params=params(60),
-        cost_estimate=cost(4 * square, 8 * length * width),
+        cost_estimate=cost(4 * square, 14 * length * width),
         name="rows_before",
     )(x, ct, *small)
     came = lax.all_to_all(send, "seq", 0, 0, tiled=True)
@@ -366,31 +339,34 @@
     )(mon_left, came)
     came_back = lax.all_to_all(send_back, "seq", 0, 0, tiled=True)
     half = shape(2 * size, 3 * LANES)
-    grad_inputs, keep, give = pl.pallas_call(
+    back_values, back_gates, keep, give = pl.pallas_call(
         functools.partial(rows_after, seq_size),
-        out_shape=(shape(length, width), half, half),
-        in_specs=[HBM] * 9,
-        out_specs=(HBM,) * 3,
+        out_shape=(cube, cube, half, half),
+        in_specs=[VMEM] * 9,
+        out_specs=(VMEM,) * 4,
         scratch_shapes=[
-            activations,
             pltpu.VMEM(half.shape, BF16),
             pltpu.VMEM(half.shape, BF16),
-            exchanged, activations, activations, *tables,
-            pltpu.VMEM((size, size), F32),
             pltpu.VMEM((size, LANES), F32),
-            exchanged, activations, activations, activations,
-            pltpu.SemaphoreType.DMA((8,)),
-            pltpu.SemaphoreType.DMA((6,)),
-            pltpu.SemaphoreType.DMA((2, 4)),
-            pltpu.SemaphoreType.DMA((4,)),
-            pltpu.SemaphoreType.DMA((2,)),
+            exchanged,
+            activations,
+            pltpu.VMEM((size, length), BF16),
+            activations,
         ],
-        compiler_params=params(60),
-        cost_estimate=cost(11 * square, 12 * length * width),
+        compiler_params=params(24),
+        cost_estimate=cost(6 * square, 16 * length * width),
         name="rows_after",
-    )(came_back, x, ct, *small, left_part)
-
-    even = lax.axis_index("seq") % 2 == 0
+    )(came_back, x, ct, values, gates, back_gated, mon_right, twiddle, left_part)
+    grad_inputs = pl.pallas_call(
+        input_grad,
+        out_shape=cube,
+        in_specs=[VMEM] * 4,
+        out_specs=VMEM,
+        compiler_params=params(20),
+        cost_estimate=cost(2 * square, 6 * length * width),
+        name="input_grad",
+    )(back_values, back_gates, w_value[0], w_gate[0])
+
     swap = [(i, i ^ 1) for i in range(seq_size)]
     like = [
         [seq * dp_size + dp for seq in range(core, seq_size, 2) for dp in range(dp_size)]
@@ -400,14 +376,27 @@
     theirs = lax.ppermute(give, "seq", swap)
     pair = (keep.astype(F32) + theirs.astype(F32)).astype(BF16)
     arrived = lax.all_to_all(pair, ("seq", "dp"), 0, 0, tiled=True, axis_index_groups=like)
-    mine = jnp.sum(arrived.reshape(peers, -1, 3 * LANES).astype(F32), axis=0)
-    factors = mine[None, :, LANES:].astype(BF16)
-    factors = jnp.broadcast_to(factors, (chan_size,) + factors.shape[1:])
-    factors = lax.all_to_all(factors, "chan", 0, 0, tiled=True).astype(F32)
-    factors = jnp.sum(factors, axis=0)
-    middle = jnp.where(even, mine[:, LANES : 2 * LANES], factors[:, :LANES])
-    done = jnp.concatenate([mine[:, :LANES], middle, factors[:, LANES:]], axis=1).astype(BF16)
-    spread = jnp.broadcast_to(done[None], (peers,) + done.shape).reshape(pair.shape)
+    rows = arrived.shape[0] // peers
+    mine, factors = pl.pallas_call(
+        sum_peers,
+        out_shape=(
+            shape(rows, 3 * LANES, dtype=F32),
+            shape(chan_size * rows, 2 * LANES),
+        ),
+        in_specs=[VMEM],
+        out_specs=(VMEM,) * 2,
+        compiler_params=params(8),
+        name="sum_peers",
+    )(arrived)
+    factors = lax.all_to_all(factors, "chan", 0, 0, tiled=True)
+    spread = pl.pallas_call(
+        sum_factors,
+        out_shape=shape(*pair.shape),
+        in_specs=[VMEM] * 2,
+        out_specs=VMEM,
+        compiler_params=params(8),
+        name="sum_factors",
+    )(mine, factors)
     half = lax.all_to_all(spread, ("seq", "dp"), 0, 0, tiled=True, axis_index_groups=like)
     other = lax.ppermute(half, "seq", swap)
     g_value, g_gate, g_out, g_right, g_left, g_twiddle = pl.pallas_call(
@@ -415,7 +404,7 @@
         out_shape=(shape(size, size, dtype=F32),) * 5 + (shape(blocks, size, dtype=F32),),
         in_specs=[VMEM] * 2,
         out_specs=(VMEM,) * 6,
-        compiler_params=params(20),
+        compiler_params=params(8),
         name="unpack",
     )(half, other)
     return grad_inputs[None], g_value[None], g_gate[None], g_out[None], g_right, g_left, g_twiddle

time: 209 us -> 202 us (0.967)
  blocking collectives: 152 us -> 176 us
  waiting for transfers between devices: 14.7 us -> 1.69 us
  starting transfers between devices: 20.5 us -> 8.53 us
  Pallas kernels: 18.2 us -> 14.3 us
    all_to_all x0 -> x1, blocking collectives: none -> 23.4 us  [on_device(): factors = lax.all_to_all(factors, 'chan', 0, 0, tiled=True)]
    all_to_all x1 -> x0, starting transfers between devices: 12.1 us -> none  [on_device(): factors = lax.all_to_all(factors, 'chan', 0, 0, tiled=True).astype(F32)]
    all_to_all x1 -> x0, waiting for transfers between devices: 11.5 us -> none  [on_device(): factors = lax.all_to_all(factors, 'chan', 0, 0, tiled=True).astype(F32)]
    pallas_call x2 -> x5, Pallas kernels: 16 us -> 12.2 us  [the longest x1 6.88 us: on_device(): pl.pallas_call(functools.partial(rows_before, seq_size), out_shape=(shape...]
  transfers between devices with their start and end apart: 3 -> 2, of which waited for: 3 -> 1; matrix products, arithmetic and copies ran while one was open for 0% -> 0% of each run, Pallas kernels for 0% -> 1%
where the time goes in v4:
time: 202 us; the launch traced here: 201 us
  blocking collectives  176 us (87%)
  Pallas kernels  14.3 us (7%)
  starting transfers between devices  8.53 us (4%)
    all_to_all x1, blocking collectives, on_device(): came = lax.all_to_all(send, 'seq', 0, 0, tiled=True)  59.8 us
    all_to_all x1, blocking collectives, on_device(): came_back = lax.all_to_all(send_back, 'seq', 0, 0, tiled=True)  54.2 us
    all_to_all x1, blocking collectives, on_device(): factors = lax.all_to_all(factors, 'chan', 0, 0, tiled=True)  23.4 us
    all_to_all x1, blocking collectives, on_device(): lax.all_to_all(pair, ('seq', 'dp'), 0, 0, tiled=True, axis_index_groups=l...  20.8 us
    all_to_all x1, blocking collectives, on_device(): lax.all_to_all(spread, ('seq', 'dp'), 0, 0, tiled=True, axis_index_groups...  17.5 us
    pallas_call x1, Pallas kernels, on_device(): pl.pallas_call(functools.partial(rows_before, seq_size), out_shape=(shape...  6.88 us
    ppermute x1, starting transfers between devices, on_device(): other = lax.ppermute(half, 'seq', swap)  6.48 us
  transfers between devices with their start and end apart: 2, of which 1 were waited for; matrix products, arithmetic and copies ran while one was open for 0% of the time, Pallas kernels for 1%

profile of v4, /device:TPU:1, one launch (start us, length us, event | category | flops | bytes accessed | tf_op | source)
XLA Modules:
  0.0 201.3 jit_solution(2128787801335210699)
XLA Ops:
  0.6 6.9 %rows_before.1 = (bf16[256,4096]{1,0:T(8,128)(2,1)}, bf16[2048,256]{1,0:T(8,128)(2,1)}, bf16[2048,256]{1,0:T(8,128)(2,1)}, bf16[2048,256]{1,0:T(8,128)(2,1)}) custom-call(bf16[2048,256]{1,0:T(8,128)(2,1)} %bitcast.27, bf16[2048,256]{1,0:T(8,128)(2,1)} %bitcast.29, bf16[256,256]{1,0:T(8,128)(2,1)} %bitcast.31, bf16[256,256]{1,0:T(8,128)(2,1)} %bitcast.33, ...), custom_call_target="tpu_custom_call" | custom-call | flops 1073741824 | bytes 7340032 | tf_op jit(solution)/shard_map/rows_before/pallas_call | solution.py:312
  7.5 0.0 copy-start.9
  7.5 59.8 %all_to_all.55 = bf16[32,8,4096]{2,1,0:T(8,128)(2,1)S(1)} all-to-all(bf16[32,8,4096]{2,1,0:T(8,128)(2,1)} %bitcast.37), channel_id=1, replica_groups=mesh['seq'=32,'chan'=4,'dp'=4] {'seq'}, dimensions={0} | all-to-all | bytes 4194304 | tf_op jit(solution)/shard_map/all_to_all | solution.py:330
  67.4 0.0 copy-done.9
  67.4 0.0 copy-start.4
  67.4 0.0 copy-start.5
  67.4 1.0 columns.1
  68.4 0.0 copy-start
  68.4 0.0 copy-start.1
  68.4 0.0 copy-start.2
  68.4 0.0 copy-start.3
  68.4 0.0 copy-start.8
  68.5 54.2 %all_to_all.56 = bf16[32,8,4096]{2,1,0:T(8,128)(2,1)S(1)} all-to-all(bf16[32,8,4096]{2,1,0:T(8,128)(2,1)S(1)} %bitcast.22), channel_id=1, replica_groups=mesh['seq'=32,'chan'=4,'dp'=4] {'seq'}, dimensions={0} | all-to-all | bytes 4194304 | tf_op jit(solution)/shard_map/all_to_all | solution.py:340
  122.7 0.0 copy-done.4
  122.7 0.0 copy-done.5
  122.7 0.0 copy-done
  122.7 0.0 copy-done.1
  122.7 0.0 copy-done.2
  122.7 0.0 copy-done.3
  122.7 0.0 copy-done.8
  122.7 3.4 %rows_after.1 = (bf16[2048,256]{1,0:T(8,128)(2,1)S(1)}, bf16[2048,256]{1,0:T(8,128)(2,1)S(1)}, bf16[512,384]{1,0:T(8,128)(2,1)S(1)}, bf16[512,384]{1,0:T(8,128)(2,1)S(1)}) custom-call(bf16[256,4096]{1,0:T(8,128)(2,1)S(1)} %bitcast.20, bf16[2048,256]{1,0:T(8,128)(2,1)S(1)} %bitcast.28, bf16[2048,256]{1,0:T(8,128)(2,1)S(1)} %bitcast.30, ...), custom_call_target="tpu_custom_call" | custom-call | flops 1610612736 | bytes 8388608 | tf_op jit(solution)/shard_map/rows_after/pallas_call | solution.py:342
  126.2 0.0 copy-start.6
  126.2 0.0 copy-start.7
  126.2 2.1 %collective-permute-start = (bf16[512,384]{1,0:T(8,128)(2,1)S(1)}, bf16[512,384]{1,0:T(8,128)(2,1)S(1)}, u32[]{:S(2)}, u32[]{:S(2)}) collective-permute-start(bf16[512,384]{1,0:T(8,128)(2,1)S(1)} %get-tuple-element.34), channel_id=1, source_target_pairs={{0,16},{16,0},{32,48},{48,32},{64,80},{80,64},{96,112},{112,96},{1... | collective-permute-start | bytes 1179656 | tf_op jit(solution)/shard_map/ppermute | solution.py:376
  128.3 1.7 collective-permute-done
  130.0 0.1 fusion
  130.1 20.8 %all_to_all.57 = bf16[64,8,384]{2,1,0:T(8,128)(2,1)S(1)} all-to-all(bf16[64,8,384]{2,1,0:T(8,128)(2,1)S(1)} %fusion), channel_id=1, replica_groups={{0,1,2,3,32,33,34,35,64,65,66,67,96,97,98,99,128,129,130,131,160,161,16..., dimensions={0} | all-to-all | bytes 786432 | tf_op jit(solution)/shard_map/all_to_all | solution.py:378
  150.9 0.1 sum_peers.1
  151.0 23.4 %all_to_all.58 = bf16[4,8,256]{2,1,0:T(8,128)(2,1)S(1)} all-to-all(bf16[4,8,256]{2,1,0:T(8,128)(2,1)S(1)} %bitcast.36), channel_id=1, replica_groups=mesh['seq'=32,'chan'=4,'dp'=4] {'chan'}, dimensions={0} | all-to-all | bytes 32768 | tf_op jit(solution)/shard_map/all_to_all | solution.py:391
  174.4 17.5 %all_to_all.59 = bf16[64,8,384]{2,1,0:T(8,128)(2,1)S(1)} all-to-all(bf16[64,8,384]{2,1,0:T(8,128)(2,1)S(1)} %bitcast.26), channel_id=1, replica_groups={{0,1,2,3,32,33,34,35,64,65,66,67,96,97,98,99,128,129,130,131,160,161,16..., dimensions={0} | all-to-all | bytes 786432 | tf_op jit(solution)/shard_map/all_to_all | solution.py:400
  192.0 6.5 %collective-permute-start.1 = (bf16[512,384]{1,0:T(8,128)(2,1)S(1)}, bf16[512,384]{1,0:T(8,128)(2,1)S(1)}, u32[]{:S(2)}, u32[]{:S(2)}) collective-permute-start(bf16[512,384]{1,0:T(8,128)(2,1)S(1)} %bitcast.23), channel_id=1, source_target_pairs={{0,16},{16,0},{32,48},{48,32},{64,80},{80,64},{96,112},{112,96},{1... | collective-permute-start | bytes 1179656 | tf_op jit(solution)/shard_map/ppermute | solution.py:401
  198.4 0.0 copy-done.6
  198.5 0.0 copy-done.7
  198.5 1.7 input_grad.1
  200.2 0.0 collective-permute-done.1.other_ref
  200.2 1.1 unpack.1
  (1 shorter events, 0.0 us)
Async XLA Ops:
  7.5 59.9 %copy-start.9 = (bf16[256,256]{1,0:T(8,128)(2,1)S(1)}, bf16[256,256]{1,0:T(8,128)(2,1)}, u32[]{:S(2)}) copy-start(bf16[256,256]{1,0:T(8,128)(2,1)} %left_ref.1) | copy-start | bytes 393220
  67.4 55.3 %copy-start.4 = (bf16[2048,256]{1,0:T(8,128)(2,1)S(1)}, bf16[2048,256]{1,0:T(8,128)(2,1)}, u32[]{:S(2)}) copy-start(bf16[2048,256]{1,0:T(8,128)(2,1)} %get-tuple-element.29.back_ref) | copy-start | bytes 3145732
  67.4 55.3 %copy-start.5 = (bf16[256,256]{1,0:T(8,128)(2,1)S(1)}, bf16[256,256]{1,0:T(8,128)(2,1)}, u32[]{:S(2)}) copy-start(bf16[256,256]{1,0:T(8,128)(2,1)} %right_ref.1) | copy-start | bytes 393220
  68.4 54.3 %copy-start = (bf16[1,2048,256]{2,1,0:T(8,128)(2,1)S(1)}, bf16[1,2048,256]{2,1,0:T(8,128)(2,1)}, u32[]{:S(2)}) copy-start(bf16[1,2048,256]{2,1,0:T(8,128)(2,1)} %param.8) | copy-start | bytes 3145732
  68.4 54.3 %copy-start.1 = (bf16[1,2048,256]{2,1,0:T(8,128)(2,1)S(1)}, bf16[1,2048,256]{2,1,0:T(8,128)(2,1)}, u32[]{:S(2)}) copy-start(bf16[1,2048,256]{2,1,0:T(8,128)(2,1)} %param.15) | copy-start | bytes 3145732
  68.4 54.3 %copy-start.2 = (bf16[2048,256]{1,0:T(8,128)(2,1)S(1)}, bf16[2048,256]{1,0:T(8,128)(2,1)}, u32[]{:S(2)}) copy-start(bf16[2048,256]{1,0:T(8,128)(2,1)} %get-tuple-element.27.value_ref) | copy-start | bytes 3145732
  68.4 54.3 %copy-start.3 = (bf16[2048,256]{1,0:T(8,128)(2,1)S(1)}, bf16[2048,256]{1,0:T(8,128)(2,1)}, u32[]{:S(2)}) copy-start(bf16[2048,256]{1,0:T(8,128)(2,1)} %get-tuple-element.28.gate_ref) | copy-start | bytes 3145732
  68.4 54.3 %copy-start.8 = (f32[8,256]{1,0:T(8,128)S(1)}, f32[8,256]{1,0:T(8,128)}, u32[]{:S(2)}) copy-start(f32[8,256]{1,0:T(8,128)} %twiddle_ref.1) | copy-start | bytes 24580
  126.2 72.3 %copy-start.6 = (bf16[1,256,256]{2,1,0:T(8,128)(2,1)S(1)}, bf16[1,256,256]{2,1,0:T(8,128)(2,1)}, u32[]{:S(2)}) copy-start(bf16[1,256,256]{2,1,0:T(8,128)(2,1)} %param.9) | copy-start | bytes 393220
  126.2 72.3 %copy-start.7 = (bf16[1,256,256]{2,1,0:T(8,128)(2,1)S(1)}, bf16[1,256,256]{2,1,0:T(8,128)(2,1)}, u32[]{:S(2)}) copy-start(bf16[1,256,256]{2,1,0:T(8,128)(2,1)} %param.10) | copy-start | bytes 393220
  126.2 3.7 %collective-permute-start = (bf16[512,384]{1,0:T(8,128)(2,1)S(1)}, bf16[512,384]{1,0:T(8,128)(2,1)S(1)}, u32[]{:S(2)}, u32[]{:S(2)}) collective-permute-start(bf16[512,384]{1,0:T(8,128)(2,1)S(1)} %get-tuple-element.34), channel_id=1, source_target_pairs={{0,16},{16,0},{32,48},{48,32},{64,80},{80,64},{96,112},{112,96},{1... | collective-permute-start | bytes 1179656 | tf_op jit(solution)/shard_map/ppermute | solution.py:376
  192.0 8.2 %collective-permute-start.1 = (bf16[512,384]{1,0:T(8,128)(2,1)S(1)}, bf16[512,384]{1,0:T(8,128)(2,1)S(1)}, u32[]{:S(2)}, u32[]{:S(2)}) collective-permute-start(bf16[512,384]{1,0:T(8,128)(2,1)S(1)} %bitcast.23), channel_id=1, source_target_pairs={{0,16},{16,0},{32,48},{48,32},{64,80},{80,64},{96,112},{112,96},{1... | collective-permute-start | bytes 1179656 | tf_op jit(solution)/shard_map/ppermute | solution.py:401

commit v5 on v4

--- a/solution.py
+++ b/solution.py
@@ -26,18 +26,9 @@
 TN = ((0,), (0,))
 
 
-def every(ref, start, count, step):
-    return ref[pl.ds(start, count, stride=step), :]
-
-
-def place_major(ref, groups, places):
-    return jnp.concatenate([every(ref, p, groups, places) for p in range(places)], axis=0)
-
-
-def group_major(ref, value, groups, places):
-    for p in range(places):
-        ref[pl.ds(p, groups, stride=places), :] = value[p * groups : (p + 1) * groups]
-    return ref[...]
+def turned_twiddle(twiddle_ref):
+    blocks, size = twiddle_ref.shape
+    return jnp.concatenate([twiddle_ref[...], jnp.zeros((LANES - blocks, size), F32)], axis=0).T
 
 
 def shuffle(outer, inner):
@@ -48,14 +39,13 @@
 
 
 def rows_before(
-    groups, x_hbm, ct_hbm, wv_hbm, wg_hbm, wo_hbm, right_hbm, twiddle_hbm,
+    x_hbm, ct_hbm, wv_hbm, wg_hbm, wo_hbm, right_hbm, twiddle_hbm,
     send_hbm, value_hbm, gate_hbm, back_hbm,
     x_ref, ct_ref, wv_ref, wg_ref, wo_ref, right_ref, twiddle_ref,
-    send_ref, value_ref, gate_ref, back_ref, wide, cols, small_sems, in_sems, out_sems, send_sems,
+    send_ref, value_ref, gate_ref, back_ref, small_sems, in_sems, out_sems, send_sems,
 ):
     blocks = twiddle_ref.shape[0]
     size = right_ref.shape[0]
-    places = size // groups
     width = x_ref.shape[1]
     parts = in_sems.shape[1]
     step = x_ref.shape[0] // parts
@@ -81,14 +71,10 @@
         )
         for copy in copies[-1]:
             copy.start()
-    to_places = shuffle(places, groups)
     for copy in small:
         copy.wait()
-    right = dot(to_places, right_ref[...]).astype(BF16)
-    wide[...] = jnp.concatenate(
-        [twiddle_ref[...], jnp.zeros((LANES - blocks, size), F32)], axis=0
-    ).T
-    twist = place_major(wide, groups, places)
+    right = right_ref[...]
+    twist = turned_twiddle(twiddle_ref)
     out = []
     for i in range(blocks):
         rows = slice(i * size, (i + 1) * size)
@@ -113,36 +99,54 @@
                 )
                 out[-1].start()
         mixed = (back.astype(F32) * gates.astype(F32)).astype(BF16)
-        mixed = dot(to_places, mixed).astype(BF16)
         twisted = (dot(right, values) * twist[:, i : i + 1]).astype(BF16)
-        for p in range(places):
-            part = slice(p * groups, (p + 1) * groups)
-            here = slice(i * groups, (i + 1) * groups)
-            cols[here, p * width : (p + 1) * width] = mixed[part]
-            cols[here, (places + p) * width : (places + p + 1) * width] = twisted[part]
-    to_send = shuffle(groups, blocks)
-    lanes = cols.shape[1] // send_sems.shape[0]
-    for n in range(send_sems.shape[0]):
-        at = slice(n * lanes, (n + 1) * lanes)
-        send_ref[:, at] = dot(to_send, cols[:, at]).astype(BF16)
-        part = pl.ds(n * lanes, lanes)
-        out.append(
-            pltpu.make_async_copy(send_ref.at[:, part], send_hbm.at[:, part], send_sems.at[n])
-        )
-        out[-1].start()
+        for k, part in enumerate((mixed, twisted)):
+            at = (k * blocks + i) * width
+            send_ref[:, at : at + width] = part
+            lanes = pl.ds(at, width)
+            out.append(
+                pltpu.make_async_copy(
+                    send_ref.at[:, lanes], send_hbm.at[:, lanes], send_sems.at[k, i]
+                )
+            )
+            out[-1].start()
     for copy in out:
         copy.wait()
 
 
-def columns(left_ref, cols_ref, send_ref, grad_ref):
-    left = left_ref[...]
-    half = cols_ref.shape[1] // 2
-    for at in range(0, half, 512):
-        back = cols_ref[:, at : at + 512]
-        twist = cols_ref[:, half + at : half + at + 512]
-        send_ref[:, at : at + 512] = dot(left, back, TN).astype(BF16)
-        send_ref[:, half + at : half + at + 512] = dot(left, twist).astype(BF16)
-    grad_ref[...] = dot(cols_ref[:, :half], cols_ref[:, half:], NT)
+def columns(
+    groups, blocks, left_ref, came_ref, send_ref, grad_ref, cols, mixed_cols, back_all, twist_all
+):
+    size = came_ref.shape[0]
+    places = size // groups
+    width = came_ref.shape[1] // (2 * blocks)
+    to_places = shuffle(places, groups)
+    to_groups = shuffle(groups, places)
+    order = shuffle(blocks, groups)
+    left = dot(order, left_ref[...]).astype(BF16)
+    left = dot(left, order, NT).astype(BF16)
+    for at in range(0, cols.shape[1], 512):
+        cols[:, at : at + 512] = dot(to_places, came_ref[:, at : at + 512]).astype(BF16)
+    for p in range(places):
+        here = slice(p * groups, (p + 1) * groups)
+        back, twist = (
+            jnp.concatenate(
+                [cols[here, (first + i) * width : (first + i + 1) * width] for i in range(blocks)],
+                axis=0,
+            )
+            for first in (0, blocks)
+        )
+        back_all[:, p * width : (p + 1) * width] = back
+        twist_all[:, p * width : (p + 1) * width] = twist
+        mixed = (dot(left, back, TN).astype(BF16), dot(left, twist).astype(BF16))
+        for k in range(2):
+            for i in range(blocks):
+                at = (k * blocks + i) * width
+                mixed_cols[here, at : at + width] = mixed[k][i * groups : (i + 1) * groups]
+    for at in range(0, cols.shape[1], 512):
+        send_ref[:, at : at + 512] = dot(to_groups, mixed_cols[:, at : at + 512]).astype(BF16)
+    grad = dot(back_all[...], twist_all[...], NT).astype(BF16)
+    grad_ref[...] = dot(dot(order, grad, TN).astype(BF16), order)
 
 
 def input_grad(back_value_ref, back_gate_ref, wv_ref, wg_ref, gi_ref):
@@ -155,49 +159,30 @@
 
 
 def rows_after(
-    groups, came_ref, x_ref, ct_ref, value_ref, gate_ref, back_ref, right_ref, twiddle_ref,
+    came_ref, x_ref, ct_ref, value_ref, gate_ref, back_ref, right_ref, twiddle_ref,
     left_grad_ref,
     back_value_ref, back_gate_ref, keep_ref, give_ref,
-    low_ref, high_ref, wide, cols, gated_all, rotated_all, turned_all,
+    low_ref, high_ref, gated_all, rotated_all, turned_all,
 ):
     size = right_ref.shape[0]
     blocks = twiddle_ref.shape[0]
-    places = size // groups
     width = x_ref.shape[1]
-    to_blocks = shuffle(blocks, groups)
-    to_groups = shuffle(groups, places)
-    right = dot(shuffle(places, groups), right_ref[...]).astype(BF16)
+    right = right_ref[...]
     right_turned = right.T
-    wide[...] = jnp.concatenate(
-        [twiddle_ref[...], jnp.zeros((LANES - blocks, size), F32)], axis=0
-    ).T
-    twist = place_major(wide, groups, places)
-    for at in range(0, cols.shape[1], 512):
-        cols[:, at : at + 512] = dot(to_blocks, came_ref[:, at : at + 512]).astype(BF16)
+    twist = turned_twiddle(twiddle_ref)
     lane = lax.broadcasted_iota(jnp.int32, (size, LANES), 1)
     twist_grad = jnp.zeros((size, LANES), F32)
     for i in range(blocks):
         rows = slice(i * size, (i + 1) * size)
-        here = slice(i * groups, (i + 1) * groups)
         values = value_ref[rows, :]
         turned_all[rows, :] = values.T
-        back, mixed = (
-            jnp.concatenate(
-                [
-                    cols[here, (first + p) * width : (first + p + 1) * width]
-                    for p in range(places)
-                ],
-                axis=0,
-            )
-            for first in (0, places)
-        )
-        back = back.astype(F32)
+        back = came_ref[:, i * width : (i + 1) * width].astype(F32)
+        mixed = came_ref[:, (blocks + i) * width : (blocks + i + 1) * width].astype(F32)
         column = jnp.sum(back * dot(right, values), axis=1, keepdims=True)
         twist_grad = jnp.where(lane == i, column, twist_grad)
         back_rotated = (back * twist[:, i : i + 1]).astype(BF16)
         rotated_all[:, rows] = back_rotated
         back_value_ref[rows, :] = dot(right_turned, back_rotated).astype(BF16)
-        mixed = dot(to_groups, mixed)
         back_gate_ref[rows, :] = (back_ref[rows, :].astype(F32) * mixed).astype(BF16)
         gated_all[rows, :] = (gate_ref[rows, :].astype(F32) * mixed).astype(BF16)
 
@@ -211,11 +196,8 @@
     put(high_ref, 0, dot(x_ref[...], back_gate_ref[...], TN))
     put(low_ref, 1, dot(gated_all[...], ct_ref[...], TN))
     put(high_ref, 2, left_grad_ref[...])
-    right_grad = dot(rotated_all[...], turned_all[...])
-    for h in range(2):
-        half = group_major(wide, right_grad[:, h * LANES : (h + 1) * LANES], groups, places)
-        low_ref[h * size : (h + 1) * size, 2 * LANES :] = half.astype(BF16)
-    flat = group_major(wide, twist_grad, groups, places).T[:blocks]
+    put(low_ref, 2, dot(rotated_all[...], turned_all[...]))
+    flat = twist_grad.T[:blocks]
     own = jnp.concatenate([flat[:, :LANES], flat[:, LANES:]], axis=0).astype(BF16)
     high_ref[:, LANES : 2 * LANES] = jnp.zeros((2 * size, LANES), BF16)
     at = pl.multiple_of(lax.axis_index("seq") * 2 * blocks, 2 * blocks)
@@ -310,18 +292,16 @@
     small = (w_value[0], w_gate[0], w_out[0], mon_right, twiddle)
     cube = shape(length, width)
     send, values, gates, back_gated = pl.pallas_call(
-        functools.partial(rows_before, seq_size),
+        rows_before,
         out_shape=(shape(seq_size * blocks, 2 * cols), cube, cube, cube),
         in_specs=[HBM] * 7,
         out_specs=(HBM,) * 4,
         scratch_shapes=[
             activations, activations, *tables, exchanged, activations, activations, activations,
-            pltpu.VMEM((size, LANES), F32),
-            exchanged,
             pltpu.SemaphoreType.DMA((5,)),
             pltpu.SemaphoreType.DMA((2, 4)),
             pltpu.SemaphoreType.DMA((3, 4)),
-            pltpu.SemaphoreType.DMA((8,)),
+            pltpu.SemaphoreType.DMA((2, blocks)),
         ],
         compiler_params=params(60),
         cost_estimate=cost(4 * square, 14 * length * width),
@@ -329,26 +309,30 @@
     )(x, ct, *small)
     came = lax.all_to_all(send, "seq", 0, 0, tiled=True)
     send_back, left_part = pl.pallas_call(
-        columns,
+        functools.partial(columns, seq_size, blocks),
         out_shape=(shape(seq_size * blocks, 2 * cols), shape(size, size, dtype=F32)),
         in_specs=[VMEM] * 2,
         out_specs=(VMEM,) * 2,
-        compiler_params=params(20),
+        scratch_shapes=[
+            exchanged,
+            exchanged,
+            pltpu.VMEM((seq_size * blocks, cols), BF16),
+            pltpu.VMEM((seq_size * blocks, cols), BF16),
+        ],
+        compiler_params=params(24),
         cost_estimate=cost(3 * square, 8 * length * width),
         name="columns",
     )(mon_left, came)
     came_back = lax.all_to_all(send_back, "seq", 0, 0, tiled=True)
     half = shape(2 * size, 3 * LANES)
     back_values, back_gates, keep, give = pl.pallas_call(
-        functools.partial(rows_after, seq_size),
+        rows_after,
         out_shape=(cube, cube, half, half),
         in_specs=[VMEM] * 9,
         out_specs=(VMEM,) * 4,
         scratch_shapes=[
             pltpu.VMEM(half.shape, BF16),
             pltpu.VMEM(half.shape, BF16),
-            pltpu.VMEM((size, LANES), F32),
-            exchanged,
             activations,
             pltpu.VMEM((size, length), BF16),
             activations,

time: 202 us -> 202 us (level)
  no operation moved by 1% of the time
where the time goes in v5:
time: 202 us; the launch traced here: 201 us
  blocking collectives  176 us (87%)
  Pallas kernels  14.1 us (7%)
  starting transfers between devices  8.53 us (4%)
    all_to_all x1, blocking collectives, on_device(): came = lax.all_to_all(send, 'seq', 0, 0, tiled=True)  59.8 us
    all_to_all x1, blocking collectives, on_device(): came_back = lax.all_to_all(send_back, 'seq', 0, 0, tiled=True)  54.2 us
    all_to_all x1, blocking collectives, on_device(): factors = lax.all_to_all(factors, 'chan', 0, 0, tiled=True)  23.4 us
    all_to_all x1, blocking collectives, on_device(): lax.all_to_all(pair, ('seq', 'dp'), 0, 0, tiled=True, axis_index_groups=l...  20.8 us
    all_to_all x1, blocking collectives, on_device(): lax.all_to_all(spread, ('seq', 'dp'), 0, 0, tiled=True, axis_index_groups...  17.5 us
    ppermute x1, starting transfers between devices, on_device(): other = lax.ppermute(half, 'seq', swap)  6.48 us
    pallas_call x1, Pallas kernels, on_device(): pl.pallas_call(rows_before, out_shape=(shape(seq_size * blocks, 2 * cols)...  5.27 us
  transfers between devices with their start and end apart: 2, of which 1 were waited for; matrix products, arithmetic and copies ran while one was open for 0% of the time, Pallas kernels for 1%

profile of v5, /device:TPU:1, one launch (start us, length us, event | category | flops | bytes accessed | tf_op | source)
XLA Modules:
  0.0 201.1 jit_solution(7520369909090401645)
XLA Ops:
  0.6 5.3 %rows_before.1 = (bf16[256,4096]{1,0:T(8,128)(2,1)}, bf16[2048,256]{1,0:T(8,128)(2,1)}, bf16[2048,256]{1,0:T(8,128)(2,1)}, bf16[2048,256]{1,0:T(8,128)(2,1)}) custom-call(bf16[2048,256]{1,0:T(8,128)(2,1)} %bitcast.27, bf16[2048,256]{1,0:T(8,128)(2,1)} %bitcast.29, bf16[256,256]{1,0:T(8,128)(2,1)} %bitcast.31, bf16[256,256]{1,0:T(8,128)(2,1)} %bitcast.33, ...), custom_call_target="tpu_custom_call" | custom-call | flops 1073741824 | bytes 7340032 | tf_op jit(solution)/shard_map/rows_before/pallas_call | solution.py:294
  5.9 0.0 copy-start.9
  5.9 59.8 %all_to_all.55 = bf16[32,8,4096]{2,1,0:T(8,128)(2,1)S(1)} all-to-all(bf16[32,8,4096]{2,1,0:T(8,128)(2,1)} %bitcast.37), channel_id=1, replica_groups=mesh['seq'=32,'chan'=4,'dp'=4] {'seq'}, dimensions={0} | all-to-all | bytes 4194304 | tf_op jit(solution)/shard_map/all_to_all | solution.py:310
  65.8 0.0 copy-done.9
  65.8 0.0 copy-start.4
  65.8 0.0 copy-start.5
  65.8 2.8 %columns.1 = (bf16[256,4096]{1,0:T(8,128)(2,1)S(1)}, f32[256,256]{1,0:T(8,128)S(1)}) custom-call(bf16[256,256]{1,0:T(8,128)(2,1)S(1)} %copy-done.9, bf16[256,4096]{1,0:T(8,128)(2,1)S(1)} %bitcast.21), custom_call_target="tpu_custom_call" | custom-call | flops 805306368 | bytes 4194304 | tf_op jit(solution)/shard_map/columns/pallas_call | solution.py:311
  68.6 0.0 copy-start
  68.6 0.0 copy-start.1
  68.6 0.0 copy-start.2
  68.6 0.0 copy-start.3
  68.6 0.0 copy-start.8
  68.7 54.2 %all_to_all.56 = bf16[32,8,4096]{2,1,0:T(8,128)(2,1)S(1)} all-to-all(bf16[32,8,4096]{2,1,0:T(8,128)(2,1)S(1)} %bitcast.22), channel_id=1, replica_groups=mesh['seq'=32,'chan'=4,'dp'=4] {'seq'}, dimensions={0} | all-to-all | bytes 4194304 | tf_op jit(solution)/shard_map/all_to_all | solution.py:326
  122.9 0.0 copy-done.4
  122.9 0.0 copy-done.5
  122.9 0.0 copy-done
  122.9 0.0 copy-done.1
  122.9 0.0 copy-done.2
  122.9 0.0 copy-done.3
  122.9 0.0 copy-done.8
  123.0 3.0 %rows_after.1 = (bf16[2048,256]{1,0:T(8,128)(2,1)S(1)}, bf16[2048,256]{1,0:T(8,128)(2,1)S(1)}, bf16[512,384]{1,0:T(8,128)(2,1)S(1)}, bf16[512,384]{1,0:T(8,128)(2,1)S(1)}) custom-call(bf16[256,4096]{1,0:T(8,128)(2,1)S(1)} %bitcast.20, bf16[2048,256]{1,0:T(8,128)(2,1)S(1)} %bitcast.28, bf16[2048,256]{1,0:T(8,128)(2,1)S(1)} %bitcast.30, ...), custom_call_target="tpu_custom_call" | custom-call | flops 1610612736 | bytes 8388608 | tf_op jit(solution)/shard_map/rows_after/pallas_call | solution.py:328
  125.9 0.0 copy-start.6
  125.9 0.0 copy-start.7
  126.0 2.1 %collective-permute-start = (bf16[512,384]{1,0:T(8,128)(2,1)S(1)}, bf16[512,384]{1,0:T(8,128)(2,1)S(1)}, u32[]{:S(2)}, u32[]{:S(2)}) collective-permute-start(bf16[512,384]{1,0:T(8,128)(2,1)S(1)} %get-tuple-element.34), channel_id=1, source_target_pairs={{0,16},{16,0},{32,48},{48,32},{64,80},{80,64},{96,112},{112,96},{1... | collective-permute-start | bytes 1179656 | tf_op jit(solution)/shard_map/ppermute | solution.py:360
  128.0 1.7 collective-permute-done
  129.7 0.1 fusion
  129.8 20.8 %all_to_all.57 = bf16[64,8,384]{2,1,0:T(8,128)(2,1)S(1)} all-to-all(bf16[64,8,384]{2,1,0:T(8,128)(2,1)S(1)} %fusion), channel_id=1, replica_groups={{0,1,2,3,32,33,34,35,64,65,66,67,96,97,98,99,128,129,130,131,160,161,16..., dimensions={0} | all-to-all | bytes 786432 | tf_op jit(solution)/shard_map/all_to_all | solution.py:362
  150.6 0.1 sum_peers.1
  150.7 23.4 %all_to_all.58 = bf16[4,8,256]{2,1,0:T(8,128)(2,1)S(1)} all-to-all(bf16[4,8,256]{2,1,0:T(8,128)(2,1)S(1)} %bitcast.36), channel_id=1, replica_groups=mesh['seq'=32,'chan'=4,'dp'=4] {'chan'}, dimensions={0} | all-to-all | bytes 32768 | tf_op jit(solution)/shard_map/all_to_all | solution.py:375
  174.2 17.5 %all_to_all.59 = bf16[64,8,384]{2,1,0:T(8,128)(2,1)S(1)} all-to-all(bf16[64,8,384]{2,1,0:T(8,128)(2,1)S(1)} %bitcast.26), channel_id=1, replica_groups={{0,1,2,3,32,33,34,35,64,65,66,67,96,97,98,99,128,129,130,131,160,161,16..., dimensions={0} | all-to-all | bytes 786432 | tf_op jit(solution)/shard_map/all_to_all | solution.py:384
  191.7 6.5 %collective-permute-start.1 = (bf16[512,384]{1,0:T(8,128)(2,1)S(1)}, bf16[512,384]{1,0:T(8,128)(2,1)S(1)}, u32[]{:S(2)}, u32[]{:S(2)}) collective-permute-start(bf16[512,384]{1,0:T(8,128)(2,1)S(1)} %bitcast.23), channel_id=1, source_target_pairs={{0,16},{16,0},{32,48},{48,32},{64,80},{80,64},{96,112},{112,96},{1... | collective-permute-start | bytes 1179656 | tf_op jit(solution)/shard_map/ppermute | solution.py:385
  198.2 0.0 copy-done.6
  198.2 0.0 copy-done.7
  198.2 1.7 input_grad.1
  200.0 0.0 collective-permute-done.1.other_ref
  200.0 1.1 unpack.1
  (1 shorter events, 0.0 us)
Async XLA Ops:
  5.9 59.9 %copy-start.9 = (bf16[256,256]{1,0:T(8,128)(2,1)S(1)}, bf16[256,256]{1,0:T(8,128)(2,1)}, u32[]{:S(2)}) copy-start(bf16[256,256]{1,0:T(8,128)(2,1)} %left_ref.1) | copy-start | bytes 393220
  65.8 57.1 %copy-start.4 = (bf16[2048,256]{1,0:T(8,128)(2,1)S(1)}, bf16[2048,256]{1,0:T(8,128)(2,1)}, u32[]{:S(2)}) copy-start(bf16[2048,256]{1,0:T(8,128)(2,1)} %get-tuple-element.29.back_ref) | copy-start | bytes 3145732
  65.8 57.1 %copy-start.5 = (bf16[256,256]{1,0:T(8,128)(2,1)S(1)}, bf16[256,256]{1,0:T(8,128)(2,1)}, u32[]{:S(2)}) copy-start(bf16[256,256]{1,0:T(8,128)(2,1)} %right_ref.1) | copy-start | bytes 393220
  68.6 54.3 %copy-start = (bf16[1,2048,256]{2,1,0:T(8,128)(2,1)S(1)}, bf16[1,2048,256]{2,1,0:T(8,128)(2,1)}, u32[]{:S(2)}) copy-start(bf16[1,2048,256]{2,1,0:T(8,128)(2,1)} %param.8) | copy-start | bytes 3145732
  68.6 54.3 %copy-start.1 = (bf16[1,2048,256]{2,1,0:T(8,128)(2,1)S(1)}, bf16[1,2048,256]{2,1,0:T(8,128)(2,1)}, u32[]{:S(2)}) copy-start(bf16[1,2048,256]{2,1,0:T(8,128)(2,1)} %param.15) | copy-start | bytes 3145732
  68.6 54.3 %copy-start.2 = (bf16[2048,256]{1,0:T(8,128)(2,1)S(1)}, bf16[2048,256]{1,0:T(8,128)(2,1)}, u32[]{:S(2)}) copy-start(bf16[2048,256]{1,0:T(8,128)(2,1)} %get-tuple-element.27.value_ref) | copy-start | bytes 3145732
  68.6 54.3 %copy-start.3 = (bf16[2048,256]{1,0:T(8,128)(2,1)S(1)}, bf16[2048,256]{1,0:T(8,128)(2,1)}, u32[]{:S(2)}) copy-start(bf16[2048,256]{1,0:T(8,128)(2,1)} %get-tuple-element.28.gate_ref) | copy-start | bytes 3145732
  68.6 54.3 %copy-start.8 = (f32[8,256]{1,0:T(8,128)S(1)}, f32[8,256]{1,0:T(8,128)}, u32[]{:S(2)}) copy-start(f32[8,256]{1,0:T(8,128)} %twiddle_ref.1) | copy-start | bytes 24580
  125.9 72.3 %copy-start.6 = (bf16[1,256,256]{2,1,0:T(8,128)(2,1)S(1)}, bf16[1,256,256]{2,1,0:T(8,128)(2,1)}, u32[]{:S(2)}) copy-start(bf16[1,256,256]{2,1,0:T(8,128)(2,1)} %param.9) | copy-start | bytes 393220
  125.9 72.3 %copy-start.7 = (bf16[1,256,256]{2,1,0:T(8,128)(2,1)S(1)}, bf16[1,256,256]{2,1,0:T(8,128)(2,1)}, u32[]{:S(2)}) copy-start(bf16[1,256,256]{2,1,0:T(8,128)(2,1)} %param.10) | copy-start | bytes 393220
  126.0 3.7 %collective-permute-start = (bf16[512,384]{1,0:T(8,128)(2,1)S(1)}, bf16[512,384]{1,0:T(8,128)(2,1)S(1)}, u32[]{:S(2)}, u32[]{:S(2)}) collective-permute-start(bf16[512,384]{1,0:T(8,128)(2,1)S(1)} %get-tuple-element.34), channel_id=1, source_target_pairs={{0,16},{16,0},{32,48},{48,32},{64,80},{80,64},{96,112},{112,96},{1... | collective-permute-start | bytes 1179656 | tf_op jit(solution)/shard_map/ppermute | solution.py:360
  191.7 8.2 %collective-permute-start.1 = (bf16[512,384]{1,0:T(8,128)(2,1)S(1)}, bf16[512,384]{1,0:T(8,128)(2,1)S(1)}, u32[]{:S(2)}, u32[]{:S(2)}) collective-permute-start(bf16[512,384]{1,0:T(8,128)(2,1)S(1)} %bitcast.23), channel_id=1, source_target_pairs={{0,16},{16,0},{32,48},{48,32},{64,80},{80,64},{96,112},{112,96},{1... | collective-permute-start | bytes 1179656 | tf_op jit(solution)/shard_map/ppermute | solution.py:385

commit v6 on v5

--- a/solution.py
+++ b/solution.py
@@ -299,8 +299,8 @@
         scratch_shapes=[
             activations, activations, *tables, exchanged, activations, activations, activations,
             pltpu.SemaphoreType.DMA((5,)),
-            pltpu.SemaphoreType.DMA((2, 4)),
-            pltpu.SemaphoreType.DMA((3, 4)),
+            pltpu.SemaphoreType.DMA((2, blocks)),
+            pltpu.SemaphoreType.DMA((3, blocks)),
             pltpu.SemaphoreType.DMA((2, blocks)),
         ],
         compiler_params=params(60),

time: 202 us -> 203 us (level)
  no operation moved by 1% of the time
where the time goes in v6:
time: 203 us
  blocking collectives  176 us (87%)
  Pallas kernels  15.6 us (8%)
  starting transfers between devices  8.53 us (4%)
    all_to_all x1, blocking collectives, on_device(): came = lax.all_to_all(send, 'seq', 0, 0, tiled=True)  59.8 us
    all_to_all x1, blocking collectives, on_device(): came_back = lax.all_to_all(send_back, 'seq', 0, 0, tiled=True)  54.2 us
    all_to_all x1, blocking collectives, on_device(): factors = lax.all_to_all(factors, 'chan', 0, 0, tiled=True)  23.4 us
    all_to_all x1, blocking collectives, on_device(): lax.all_to_all(pair, ('seq', 'dp'), 0, 0, tiled=True, axis_index_groups=l...  20.8 us
    all_to_all x1, blocking collectives, on_device(): lax.all_to_all(spread, ('seq', 'dp'), 0, 0, tiled=True, axis_index_groups...  17.5 us
    pallas_call x1, Pallas kernels, on_device(): pl.pallas_call(rows_before, out_shape=(shape(seq_size * blocks, 2 * cols)...  6.83 us
    ppermute x1, starting transfers between devices, on_device(): other = lax.ppermute(half, 'seq', swap)  6.48 us
  transfers between devices with their start and end apart: 2, of which 1 were waited for; matrix products, arithmetic and copies ran while one was open for 0% of the time, Pallas kernels for 1%

profile of v6, /device:TPU:1, one launch (start us, length us, event | category | flops | bytes accessed | tf_op | source)
XLA Modules:
  0.0 202.7 jit_solution(8767620259216982938)
XLA Ops:
  0.6 6.8 %rows_before.1 = (bf16[256,4096]{1,0:T(8,128)(2,1)}, bf16[2048,256]{1,0:T(8,128)(2,1)}, bf16[2048,256]{1,0:T(8,128)(2,1)}, bf16[2048,256]{1,0:T(8,128)(2,1)}) custom-call(bf16[2048,256]{1,0:T(8,128)(2,1)} %bitcast.27, bf16[2048,256]{1,0:T(8,128)(2,1)} %bitcast.29, bf16[256,256]{1,0:T(8,128)(2,1)} %bitcast.31, bf16[256,256]{1,0:T(8,128)(2,1)} %bitcast.33, ...), custom_call_target="tpu_custom_call" | custom-call | flops 1073741824 | bytes 7340032 | tf_op jit(solution)/shard_map/rows_before/pallas_call | solution.py:294
  7.5 0.0 copy-start.9
  7.5 59.8 %all_to_all.55 = bf16[32,8,4096]{2,1,0:T(8,128)(2,1)S(1)} all-to-all(bf16[32,8,4096]{2,1,0:T(8,128)(2,1)} %bitcast.37), channel_id=1, replica_groups=mesh['seq'=32,'chan'=4,'dp'=4] {'seq'}, dimensions={0} | all-to-all | bytes 4194304 | tf_op jit(solution)/shard_map/all_to_all | solution.py:310
  67.3 0.0 copy-done.9
  67.3 0.0 copy-start.4
  67.3 0.0 copy-start.5
  67.3 2.8 %columns.1 = (bf16[256,4096]{1,0:T(8,128)(2,1)S(1)}, f32[256,256]{1,0:T(8,128)S(1)}) custom-call(bf16[256,256]{1,0:T(8,128)(2,1)S(1)} %copy-done.9, bf16[256,4096]{1,0:T(8,128)(2,1)S(1)} %bitcast.21), custom_call_target="tpu_custom_call" | custom-call | flops 805306368 | bytes 4194304 | tf_op jit(solution)/shard_map/columns/pallas_call | solution.py:311
  70.2 0.0 copy-start
  70.2 0.0 copy-start.1
  70.2 0.0 copy-start.2
  70.2 0.0 copy-start.3
  70.2 0.0 copy-start.8
  70.2 54.2 %all_to_all.56 = bf16[32,8,4096]{2,1,0:T(8,128)(2,1)S(1)} all-to-all(bf16[32,8,4096]{2,1,0:T(8,128)(2,1)S(1)} %bitcast.22), channel_id=1, replica_groups=mesh['seq'=32,'chan'=4,'dp'=4] {'seq'}, dimensions={0} | all-to-all | bytes 4194304 | tf_op jit(solution)/shard_map/all_to_all | solution.py:326
  124.4 0.0 copy-done.4
  124.5 0.0 copy-done.5
  124.5 0.0 copy-done
  124.5 0.0 copy-done.1
  124.5 0.0 copy-done.2
  124.5 0.0 copy-done.3
  124.5 0.0 copy-done.8
  124.5 3.0 %rows_after.1 = (bf16[2048,256]{1,0:T(8,128)(2,1)S(1)}, bf16[2048,256]{1,0:T(8,128)(2,1)S(1)}, bf16[512,384]{1,0:T(8,128)(2,1)S(1)}, bf16[512,384]{1,0:T(8,128)(2,1)S(1)}) custom-call(bf16[256,4096]{1,0:T(8,128)(2,1)S(1)} %bitcast.20, bf16[2048,256]{1,0:T(8,128)(2,1)S(1)} %bitcast.28, bf16[2048,256]{1,0:T(8,128)(2,1)S(1)} %bitcast.30, ...), custom_call_target="tpu_custom_call" | custom-call | flops 1610612736 | bytes 8388608 | tf_op jit(solution)/shard_map/rows_after/pallas_call | solution.py:328
  127.5 0.0 copy-start.6
  127.5 0.0 copy-start.7
  127.5 2.1 %collective-permute-start = (bf16[512,384]{1,0:T(8,128)(2,1)S(1)}, bf16[512,384]{1,0:T(8,128)(2,1)S(1)}, u32[]{:S(2)}, u32[]{:S(2)}) collective-permute-start(bf16[512,384]{1,0:T(8,128)(2,1)S(1)} %get-tuple-element.34), channel_id=1, source_target_pairs={{0,16},{16,0},{32,48},{48,32},{64,80},{80,64},{96,112},{112,96},{1... | collective-permute-start | bytes 1179656 | tf_op jit(solution)/shard_map/ppermute | solution.py:360
  129.6 1.7 collective-permute-done
  131.3 0.1 fusion
  131.4 20.8 %all_to_all.57 = bf16[64,8,384]{2,1,0:T(8,128)(2,1)S(1)} all-to-all(bf16[64,8,384]{2,1,0:T(8,128)(2,1)S(1)} %fusion), channel_id=1, replica_groups={{0,1,2,3,32,33,34,35,64,65,66,67,96,97,98,99,128,129,130,131,160,161,16..., dimensions={0} | all-to-all | bytes 786432 | tf_op jit(solution)/shard_map/all_to_all | solution.py:362
  152.2 0.1 sum_peers.1
  152.3 23.4 %all_to_all.58 = bf16[4,8,256]{2,1,0:T(8,128)(2,1)S(1)} all-to-all(bf16[4,8,256]{2,1,0:T(8,128)(2,1)S(1)} %bitcast.36), channel_id=1, replica_groups=mesh['seq'=32,'chan'=4,'dp'=4] {'chan'}, dimensions={0} | all-to-all | bytes 32768 | tf_op jit(solution)/shard_map/all_to_all | solution.py:375
  175.7 17.5 %all_to_all.59 = bf16[64,8,384]{2,1,0:T(8,128)(2,1)S(1)} all-to-all(bf16[64,8,384]{2,1,0:T(8,128)(2,1)S(1)} %bitcast.26), channel_id=1, replica_groups={{0,1,2,3,32,33,34,35,64,65,66,67,96,97,98,99,128,129,130,131,160,161,16..., dimensions={0} | all-to-all | bytes 786432 | tf_op jit(solution)/shard_map/all_to_all | solution.py:384
  193.3 6.5 %collective-permute-start.1 = (bf16[512,384]{1,0:T(8,128)(2,1)S(1)}, bf16[512,384]{1,0:T(8,128)(2,1)S(1)}, u32[]{:S(2)}, u32[]{:S(2)}) collective-permute-start(bf16[512,384]{1,0:T(8,128)(2,1)S(1)} %bitcast.23), channel_id=1, source_target_pairs={{0,16},{16,0},{32,48},{48,32},{64,80},{80,64},{96,112},{112,96},{1... | collective-permute-start | bytes 1179656 | tf_op jit(solution)/shard_map/ppermute | solution.py:385
  199.8 0.0 copy-done.6
  199.8 0.0 copy-done.7
  199.8 1.7 input_grad.1
  201.5 0.0 collective-permute-done.1.other_ref
  201.5 1.1 unpack.1
  (1 shorter events, 0.0 us)
Async XLA Ops:
  7.5 59.9 %copy-start.9 = (bf16[256,256]{1,0:T(8,128)(2,1)S(1)}, bf16[256,256]{1,0:T(8,128)(2,1)}, u32[]{:S(2)}) copy-start(bf16[256,256]{1,0:T(8,128)(2,1)} %left_ref.1) | copy-start | bytes 393220
  67.3 57.1 %copy-start.4 = (bf16[2048,256]{1,0:T(8,128)(2,1)S(1)}, bf16[2048,256]{1,0:T(8,128)(2,1)}, u32[]{:S(2)}) copy-start(bf16[2048,256]{1,0:T(8,128)(2,1)} %get-tuple-element.29.back_ref) | copy-start | bytes 3145732
  67.3 57.1 %copy-start.5 = (bf16[256,256]{1,0:T(8,128)(2,1)S(1)}, bf16[256,256]{1,0:T(8,128)(2,1)}, u32[]{:S(2)}) copy-start(bf16[256,256]{1,0:T(8,128)(2,1)} %right_ref.1) | copy-start | bytes 393220
  70.2 54.3 %copy-start = (bf16[1,2048,256]{2,1,0:T(8,128)(2,1)S(1)}, bf16[1,2048,256]{2,1,0:T(8,128)(2,1)}, u32[]{:S(2)}) copy-start(bf16[1,2048,256]{2,1,0:T(8,128)(2,1)} %param.8) | copy-start | bytes 3145732
  70.2 54.3 %copy-start.1 = (bf16[1,2048,256]{2,1,0:T(8,128)(2,1)S(1)}, bf16[1,2048,256]{2,1,0:T(8,128)(2,1)}, u32[]{:S(2)}) copy-start(bf16[1,2048,256]{2,1,0:T(8,128)(2,1)} %param.15) | copy-start | bytes 3145732
  70.2 54.3 %copy-start.2 = (bf16[2048,256]{1,0:T(8,128)(2,1)S(1)}, bf16[2048,256]{1,0:T(8,128)(2,1)}, u32[]{:S(2)}) copy-start(bf16[2048,256]{1,0:T(8,128)(2,1)} %get-tuple-element.27.value_ref) | copy-start | bytes 3145732
  70.2 54.3 %copy-start.3 = (bf16[2048,256]{1,0:T(8,128)(2,1)S(1)}, bf16[2048,256]{1,0:T(8,128)(2,1)}, u32[]{:S(2)}) copy-start(bf16[2048,256]{1,0:T(8,128)(2,1)} %get-tuple-element.28.gate_ref) | copy-start | bytes 3145732
  70.2 54.3 %copy-start.8 = (f32[8,256]{1,0:T(8,128)S(1)}, f32[8,256]{1,0:T(8,128)}, u32[]{:S(2)}) copy-start(f32[8,256]{1,0:T(8,128)} %twiddle_ref.1) | copy-start | bytes 24580
  127.5 72.3 %copy-start.6 = (bf16[1,256,256]{2,1,0:T(8,128)(2,1)S(1)}, bf16[1,256,256]{2,1,0:T(8,128)(2,1)}, u32[]{:S(2)}) copy-start(bf16[1,256,256]{2,1,0:T(8,128)(2,1)} %param.9) | copy-start | bytes 393220
  127.5 72.3 %copy-start.7 = (bf16[1,256,256]{2,1,0:T(8,128)(2,1)S(1)}, bf16[1,256,256]{2,1,0:T(8,128)(2,1)}, u32[]{:S(2)}) copy-start(bf16[1,256,256]{2,1,0:T(8,128)(2,1)} %param.10) | copy-start | bytes 393220
  127.5 3.7 %collective-permute-start = (bf16[512,384]{1,0:T(8,128)(2,1)S(1)}, bf16[512,384]{1,0:T(8,128)(2,1)S(1)}, u32[]{:S(2)}, u32[]{:S(2)}) collective-permute-start(bf16[512,384]{1,0:T(8,128)(2,1)S(1)} %get-tuple-element.34), channel_id=1, source_target_pairs={{0,16},{16,0},{32,48},{48,32},{64,80},{80,64},{96,112},{112,96},{1... | collective-permute-start | bytes 1179656 | tf_op jit(solution)/shard_map/ppermute | solution.py:360
  193.3 8.2 %collective-permute-start.1 = (bf16[512,384]{1,0:T(8,128)(2,1)S(1)}, bf16[512,384]{1,0:T(8,128)(2,1)S(1)}, u32[]{:S(2)}, u32[]{:S(2)}) collective-permute-start(bf16[512,384]{1,0:T(8,128)(2,1)S(1)} %bitcast.23), channel_id=1, source_target_pairs={{0,16},{16,0},{32,48},{48,32},{64,80},{80,64},{96,112},{112,96},{1... | collective-permute-start | bytes 1179656 | tf_op jit(solution)/shard_map/ppermute | solution.py:385
